TPU v7x, 512 devices: a whole 4x8x8 slice. The times are simulated.
512 devices in a mesh: ctx: 8 (over y), exp: 64 (over x, z, core).
Axes of the slice: x: 4, y: 8, z: 8, core: 2. Of those that a mesh axis runs over, the one named last changes fastest.
Arguments:
- hidden_rows: bfloat16 [65536, 1440], P(('ctx', 'exp')), may hold values from -6 to 6
- queries: bfloat16 [65536, 2048], P(('ctx', 'exp')), may hold values from -7 to 7
- keys: bfloat16 [65536, 256], P(('ctx', 'exp')), may hold values from -7 to 7
- values: bfloat16 [65536, 256], P(('ctx', 'exp')), may hold values from -6 to 6
- sinks: float32 [32], replicated, may hold values from 0 to 5
- norm_gain: float32 [1440], replicated, may hold values from 0.1 to 1.9
- learner_row: int32 [65536], P(('ctx', 'exp')), may hold values from 0 to 65535, as said below
- expert_ids: int32 [65536, 2], P(('ctx', 'exp')), may hold values from 0 to 63, all different within a row; in each aligned block of 128 rows (0 to 127, 128 to 255, ...) at most 8 rows name the same one
- route_weight: float32 [65536, 2], P(('ctx', 'exp')), may hold values from 0.1 to 1
- gate_w: bfloat16 [64, 1440, 1440], P('exp', 'ctx'), may hold values from -0.15625 to 0.15625
- up_w: bfloat16 [64, 1440, 1440], P('exp', 'ctx'), may hold values from -0.15625 to 0.15625
- down_w: bfloat16 [64, 1440, 1440], P('exp', 'ctx'), may hold values from -0.15625 to 0.15625
Outputs:
- attn_rows: bfloat16 [65536, 2048], P(('ctx', 'exp'))
- mixed: bfloat16 [65536, 1440], P(('ctx', 'exp'))
Inputs may be any that keep to these rules, and one draw needn't show every extreme that they name: `learner_row`: A permutation of the rows. Every row stays within its block of 8192 rows; within such a block, the learner rows of device d of a block whose offset within d's 128 rows lies in [s * 2, (s + 1) * 2) come from the rollout rows of device s of that block. `expert_ids`: each row names 2 different experts. Among the 128 rows of one device no expert is named more than 8 times; some device names some expert exactly 8 times.
All inputs are finite; a program needn't handle non-finite values.
Results may differ from a plain program's by a relative error of at most 0.0053.
Values may be sent and summed in bfloat16 or wider, within the bound.
No kernel may reach another device: no remote copies, remote signals or barrier semaphores. Data moves between devices by JAX's collectives and lax.ppermute only.
A program may use at most 128 MiB of HBM per device.

v0:
```python
import math

import jax
import jax.numpy as jnp
from jax import lax
from jax.experimental import pallas as pl
from jax.experimental.pallas import tpu as pltpu
from jax.sharding import PartitionSpec as P

D = 1440
FFW = 1440
QHEADS = 32
KVHEADS = 4
HEAD = 64
WINDOW = 128
ROUTES = 2
CAP = 8
LANES = 128
PANEL = 512
VMEM_BYTES = 60 * 1024 * 1024


def shifted(block, axis, distance):
    devices = range(lax.axis_size(axis))
    route = [(i - distance, i) for i in devices if i - distance in devices]
    return lax.ppermute(block, axis, route)


def pick_rows(choice, rows):
    return jnp.dot(choice, rows, preferred_element_type=jnp.float32).astype(jnp.bfloat16)


def panels(width):
    return [(low, min(low + PANEL, width)) for low in range(0, width, PANEL)]


def experts_kernel(rows_ref, wide_ref, out_ref, sliced, wide, total, hidden, arrival):
    count, depth = wide_ref.shape[0], wide_ref.shape[1]
    width = rows_ref.shape[1]
    copies = [
        pltpu.make_async_copy(wide_ref.at[s], wide.at[s], arrival.at[s]) for s in range(count)
    ]
    for copy in copies:
        copy.start()
    for s in range(count):
        sliced[s] = rows_ref[:, s * depth : (s + 1) * depth]
    for s in range(count):
        copies[s].wait()
        for low, high in panels(total.shape[1]):
            part = jnp.dot(sliced[s], wide[s, :, low:high], preferred_element_type=jnp.float32)
            total[:, low:high] = part if s == 0 else total[:, low:high] + part
    for low, high in panels(width):
        hidden[:, low:high] = gated_hidden(
            total[:, low:high], total[:, width + low : width + high]
        )
    for s in range(count):
        sliced[s] = hidden[:, s * depth : (s + 1) * depth]
    start = 2 * width // LANES * LANES
    for low, high in panels(3 * width - start):
        part = jnp.dot(
            sliced[0], wide[0, :, start + low : start + high], preferred_element_type=jnp.float32
        )
        for s in range(1, count):
            part += jnp.dot(
                sliced[s],
                wide[s, :, start + low : start + high],
                preferred_element_type=jnp.float32,
            )
        total[:, low:high] = part
    lead = 2 * width - start
    out_ref[...] = total[:, lead : lead + width].astype(jnp.bfloat16)


def experts_call(rows, wide_all):
    count, depth, _ = wide_all.shape
    slots, width = rows.shape
    whole = pl.BlockSpec(memory_space=pltpu.VMEM)
    return pl.pallas_call(
        experts_kernel,
        out_shape=jax.ShapeDtypeStruct((slots, width), jnp.bfloat16),
        in_specs=[whole, pl.BlockSpec(memory_space=pltpu.HBM)],
        out_specs=whole,
        scratch_shapes=[
            pltpu.VMEM((count, slots, depth), jnp.bfloat16),
            pltpu.VMEM(wide_all.shape, jnp.bfloat16),
            pltpu.VMEM((slots, -(-2 * width // LANES) * LANES), jnp.float32),
            pltpu.VMEM((slots, width), jnp.bfloat16),
            pltpu.SemaphoreType.DMA((count,)),
        ],
        compiler_params=pltpu.CompilerParams(vmem_limit_bytes=VMEM_BYTES),
        cost_estimate=pl.CostEstimate(
            flops=6 * slots * width * width,
            bytes_accessed=6 * width * width + 4 * slots * width,
            transcendentals=slots * width,
        ),
    )(rows, wide_all)


def exchange(rows, peer_count):
    parts = rows.reshape(peer_count, -1, rows.shape[1])
    return lax.all_to_all(parts, "exp", split_axis=0, concat_axis=0, tiled=True).reshape(rows.shape)


def gated_hidden(gate, upward):
    return (gate * jax.nn.sigmoid(1.702 * gate) * (upward + 1.0)).astype(jnp.bfloat16)


def attend(query_rows, key_value_rows, sinks):
    tokens_here = query_rows.shape[0]
    previous = shifted(key_value_rows, ("ctx", "exp"), 1)
    span_rows = WINDOW + tokens_here
    groups = QHEADS // KVHEADS
    span = jnp.concatenate([previous, key_value_rows], 0)
    all_keys = span[:, : KVHEADS * HEAD].reshape(span_rows, KVHEADS, HEAD)
    all_values = span[:, KVHEADS * HEAD :].reshape(span_rows, KVHEADS, HEAD)
    query_heads = query_rows.reshape(tokens_here, KVHEADS, groups, HEAD)
    scores = jnp.einsum(
        "ihgd,jhd->hgij", query_heads, all_keys, preferred_element_type=jnp.float32
    ) * (1.0 / math.sqrt(HEAD))
    first_row = lax.axis_index(("ctx", "exp")) * tokens_here
    query_place = first_row + jnp.arange(tokens_here, dtype=jnp.int32)
    key_place = first_row - WINDOW + jnp.arange(span_rows, dtype=jnp.int32)
    distance = query_place[:, None] - key_place[None, :]
    allowed = (distance >= 0) & (distance < WINDOW) & (key_place >= 0)[None, :]
    scores = jnp.where(allowed, scores, -1e30)
    sink_logit = sinks.reshape(KVHEADS, groups)[:, :, None]
    row_max = jnp.maximum(jnp.max(scores, -1), sink_logit)
    expo_terms = jnp.exp(scores - row_max[..., None])
    denom_total = jnp.sum(expo_terms, -1) + jnp.exp(sink_logit - row_max)
    probs = (expo_terms / denom_total[..., None]).astype(jnp.bfloat16)
    attended = jnp.einsum("hgij,jhd->ihgd", probs, all_values, preferred_element_type=jnp.float32)
    return attended.reshape(tokens_here, QHEADS * HEAD).astype(jnp.bfloat16)


def per_device(
    hidden_rows,
    queries,
    keys,
    values,
    sinks,
    norm_gain,
    learner_row,
    expert_ids,
    route_weight,
    gate_w,
    up_w,
    down_w,
):
    tokens_here = hidden_rows.shape[0]
    peer_count = lax.axis_size("exp")
    per_peer = tokens_here // peer_count
    gate_block, up_block, down_block = gate_w[0], up_w[0], down_w[0]

    wide_all = lax.all_gather(
        jnp.concatenate([gate_block, up_block, down_block], 1), "ctx", axis=0
    )

    slot = learner_row % (peer_count * tokens_here) // tokens_here * per_peer + learner_row % per_peer
    order = (jnp.arange(tokens_here, dtype=jnp.int32)[:, None] == slot[None, :]).astype(jnp.bfloat16)
    resid = exchange(pick_rows(order, hidden_rows), peer_count)
    resid_float = resid.astype(jnp.float32)
    mean_square = jnp.mean(resid_float * resid_float, -1, keepdims=True)
    normed = (resid_float * lax.rsqrt(mean_square + 1e-05) * norm_gain).astype(jnp.bfloat16)

    slots_total = peer_count * CAP
    pair_count = tokens_here * ROUTES
    pair_expert = expert_ids.reshape(-1)
    hits = pair_expert[:, None] == jnp.arange(peer_count, dtype=jnp.int32)[None, :]
    pair_place = jnp.arange(pair_count, dtype=jnp.int32)
    before = (pair_place[:, None] > pair_place[None, :]).astype(jnp.bfloat16)
    earlier = jnp.dot(before, hits.astype(jnp.bfloat16), preferred_element_type=jnp.float32)
    pair_rank = jnp.sum(jnp.where(hits, earlier, 0.0), 1).astype(jnp.int32)
    slot_index = (pair_expert * CAP + pair_rank).reshape(tokens_here, ROUTES)
    slots = jnp.arange(slots_total, dtype=jnp.int32)
    sent = sum(slots[:, None] == slot_index[None, :, r] for r in range(ROUTES))
    outgoing = pick_rows(sent.astype(jnp.bfloat16), normed)
    expert_rows = exchange(outgoing, peer_count)
    packed = jnp.concatenate([queries, keys, values], 1)
    expert_rows, packed = lax.optimization_barrier((expert_rows, packed))
    arrived = exchange(pick_rows(order, packed), peer_count)
    query_rows = arrived[:, : QHEADS * HEAD]
    key_value_rows = arrived[:, QHEADS * HEAD :]
    weight_high = lax.reduce_precision(route_weight, 8, 7)
    weight_low = route_weight - weight_high

    def selection(weight):
        return sum(
            jnp.where(slots[None, :] == slot_index[:, r, None], weight[:, r, None], 0.0)
            for r in range(ROUTES)
        ).astype(jnp.bfloat16)

    combine = jnp.concatenate([selection(weight_high), selection(weight_low)], 0)

    attn_rows = attend(query_rows, key_value_rows, sinks)

    expert_out = experts_call(expert_rows, wide_all)
    returned = exchange(expert_out, peer_count)
    both = jnp.dot(combine, returned, preferred_element_type=jnp.float32)
    total = both[:tokens_here] + both[tokens_here:]
    return (attn_rows, (resid_float + total).astype(jnp.bfloat16))


def solution(mesh):
    return jax.shard_map(
        per_device,
        mesh=mesh,
        in_specs=(
            P(("ctx", "exp"), None),
            P(("ctx", "exp"), None),
            P(("ctx", "exp"), None),
            P(("ctx", "exp"), None),
            P(),
            P(),
            P(("ctx", "exp")),
            P(("ctx", "exp"), None),
            P(("ctx", "exp"), None),
            P("exp", "ctx", None),
            P("exp", "ctx", None),
            P("exp", "ctx", None),
        ),
        out_specs=(P(("ctx", "exp"), None), P(("ctx", "exp"), None)),
        check_vma=False,
    )
```

profile of v0, /device:TPU:6, one launch (start us, length us, event | category | flops | bytes accessed | tf_op | source)
XLA Modules:
  0.0 233.5 jit_solution(420214311389777058)
XLA Ops:
  7.2 4.2 %concatenate.15 = bf16[180,4320]{1,0:T(8,128)(2,1)} concatenate(bf16[180,1440]{1,0:T(8,128)(2,1)} %bitcast.56, bf16[180,1440]{1,0:T(8,128)(2,1)} %bitcast.57, bf16[180,1440]{1,0:T(8,128)(2,1)} %bitcast.58), dimensions={1} | concatenate | bytes 3110400 | tf_op jit(solution)/shard_map/concatenate | solution.py:155
  12.0 0.9 reshape.87
  12.9 14.0 %all-to-all-start = ((bf16[64,2,1440]{2,1,0:T(2,128)(2,1)}), bf16[64,2,1440]{2,1,0:T(2,128)(2,1)S(1)}, u32[]{:S(2)}, u32[]{:S(2)}) async-start(bf16[64,2,1440]{2,1,0:T(2,128)(2,1)} %reshape.87), calls=%async_computation | async-start | bytes 786432 | tf_op jit(solution)/shard_map/all_to_all | solution.py:101
  27.6 13.4 %all-to-all-done = bf16[64,2,1440]{2,1,0:T(2,128)(2,1)S(1)} async-done(((bf16[64,2,1440]{2,1,0:T(2,128)(2,1)}), bf16[64,2,1440]{2,1,0:T(2,128)(2,1)S(1)}, u32[]{:S(2)}, u32[]{:S(2)}) %all-to-all-start) | async-done | bytes 368672 | tf_op jit(solution)/shard_map/all_to_all | solution.py:101
  41.0 0.5 multiply_reduce_fusion
  42.0 0.7 convolution_convert_fusion.1
  42.6 1.6 copy.52
  44.2 6.8 %all-to-all-start.1 = ((bf16[64,8,1440]{2,1,0:T(8,128)(2,1)}), bf16[64,8,1440]{2,1,0:T(8,128)(2,1)S(1)}, u32[]{:S(2)}, u32[]{:S(2)}) async-start(bf16[64,8,1440]{2,1,0:T(8,128)(2,1)} %bitcast.2), calls=%async_computation.1 | async-start | bytes 3145728 | tf_op jit(solution)/shard_map/all_to_all | solution.py:101
  51.0 1.1 pad_maximum_fusion
  52.1 36.5 %all-to-all-done.1 = bf16[64,8,1440]{2,1,0:T(8,128)(2,1)S(1)} async-done(((bf16[64,8,1440]{2,1,0:T(8,128)(2,1)}), bf16[64,8,1440]{2,1,0:T(8,128)(2,1)S(1)}, u32[]{:S(2)}, u32[]{:S(2)}) %all-to-all-start.1) | async-done | bytes 1474592 | tf_op jit(solution)/shard_map/all_to_all | solution.py:101
  88.6 1.2 copy-done.1
  89.8 0.3 convolution_convert_fusion
  90.1 1.1 reshape.90
  91.2 8.3 %all-to-all-start.2 = ((bf16[64,2,2560]{2,1,0:T(2,128)(2,1)}), bf16[64,2,2560]{2,1,0:T(2,128)(2,1)S(1)}, u32[]{:S(2)}, u32[]{:S(2)}) async-start(bf16[64,2,2560]{2,1,0:T(2,128)(2,1)} %reshape.90), calls=%async_computation.2 | async-start | bytes 1310720 | tf_op jit(solution)/shard_map/all_to_all | solution.py:101
  99.7 54.5 %all-gather.4.cloned.1.call-done.wide_ref = bf16[8,180,4320]{2,1,0:T(8,128)(2,1)} async-done(((bf16[1,180,4320]{2,1,0:T(8,128)(2,1)}), bf16[8,180,4320]{2,1,0:T(8,128)(2,1)}) %all-gather.4.cloned.1.call-update) | async-done | bytes 12441616 | tf_op jit(solution)/shard_map/all_gather | solution.py:154
  154.1 15.9 %shard_map.131 = bf16[512,1440]{1,0:T(8,128)(2,1)} custom-call(bf16[512,1440]{1,0:T(8,128)(2,1)} %bitcast.55, bf16[8,180,4320]{2,1,0:T(8,128)(2,1)} %all-gather.4.cloned.1.call-done.wide_ref), custom_call_target="tpu_custom_call" | custom-call | flops 6370099200 | bytes 15390720 | tf_op jit(solution)/shard_map/pallas_call | solution.py:78
  170.1 11.1 %all-to-all-start.3 = ((bf16[64,8,1440]{2,1,0:T(8,128)(2,1)}), bf16[64,8,1440]{2,1,0:T(8,128)(2,1)S(1)}, u32[]{:S(2)}, u32[]{:S(2)}) async-start(bf16[64,8,1440]{2,1,0:T(8,128)(2,1)} %bitcast.54), calls=%async_computation.3 | async-start | bytes 3145728 | tf_op jit(solution)/shard_map/all_to_all | solution.py:101
  181.3 0.9 add_convert_fusion.1
  182.1 1.1 reshape.91
  183.2 0.9 slice.52
  184.1 0.8 copy.61
  184.9 2.0 collective-permute-start
  187.4 1.9 slice.55
  189.2 1.3 copy.62
  190.6 29.4 %collective-permute-done = bf16[128,512]{0,1:T(8,128)(2,1)} collective-permute-done((bf16[128,512]{0,1:T(8,128)(2,1)}, bf16[128,512]{0,1:T(8,128)(2,1)}, u32[]{:S(2)}, u32[]{:S(2)}) %collective-permute-start) | collective-permute-done | bytes 131104 | tf_op jit(solution)/shard_map/ppermute | solution.py:26
  220.0 1.0 pad_maximum_fusion.1
  220.9 0.8 fusion.1
  221.8 0.9 fusion
  222.8 1.2 fusion.5
  223.9 1.0 copy.57
  225.0 0.8 fusion.3
  225.7 0.9 fusion.8
  (49 shorter events, 2.3 us)
Async XLA Ops:
  7.2 4.3 %copy-start = (bf16[128,1440]{0,1:T(8,128)(2,1)S(1)}, bf16[128,1440]{0,1:T(8,128)(2,1)}, u32[]{:S(2)}) copy-start(bf16[128,1440]{0,1:T(8,128)(2,1)} %param.12) | copy-start | bytes 1105924
  7.2 4.3 %copy-start.10 = (s32[128]{0:T(128)S(1)}, s32[128]{0:T(128)}, u32[]{:S(2)}) copy-start(s32[128]{0:T(128)} %param.18) | copy-start | bytes 1540
  7.2 19.7 %copy-start.7 = (s32[128,2]{0,1:T(2,128)S(1)}, s32[128,2]{0,1:T(2,128)}, u32[]{:S(2)}) copy-start(s32[128,2]{0,1:T(2,128)} %param.19) | copy-start | bytes 3076
  7.2 146.9 %all-gather.4.cloned.1.call-start = ((), (), s32[]{:S(2)}) async-start(), calls=%async_computation.4 | async-start | bytes 14413824 | tf_op jit(solution)/shard_map/all_gather | solution.py:154
  11.4 30.5 %copy-start.6 = (f32[1440]{0:T(1024)S(1)}, f32[1440]{0:T(1024)}, u32[]{:S(2)}) copy-start(f32[1440]{0:T(1024)} %param.17) | copy-start | bytes 17284
  12.9 28.2 %all-to-all-start = ((bf16[64,2,1440]{2,1,0:T(2,128)(2,1)}), bf16[64,2,1440]{2,1,0:T(2,128)(2,1)S(1)}, u32[]{:S(2)}, u32[]{:S(2)}) async-start(bf16[64,2,1440]{2,1,0:T(2,128)(2,1)} %reshape.87), calls=%async_computation | async-start | bytes 786432 | tf_op jit(solution)/shard_map/all_to_all | solution.py:101
  41.9 9.1 %copy-start.4 = (bf16[128,256]{1,0:T(8,128)(2,1)S(1)}, bf16[128,256]{1,0:T(8,128)(2,1)}, u32[]{:S(2)}) copy-start(bf16[128,256]{1,0:T(8,128)(2,1)} %param.15) | copy-start | bytes 196612
  41.9 9.1 %copy-start.5 = (bf16[128,256]{1,0:T(8,128)(2,1)S(1)}, bf16[128,256]{1,0:T(8,128)(2,1)}, u32[]{:S(2)}) copy-start(bf16[128,256]{1,0:T(8,128)(2,1)} %param.14) | copy-start | bytes 196612
  44.2 55.3 %copy-start.9 = (f32[32]{0:T(128)S(1)}, f32[32]{0:T(128)}, u32[]{:S(2)}) copy-start(f32[32]{0:T(128)} %param.16) | copy-start | bytes 388
  44.2 44.4 %all-to-all-start.1 = ((bf16[64,8,1440]{2,1,0:T(8,128)(2,1)}), bf16[64,8,1440]{2,1,0:T(8,128)(2,1)S(1)}, u32[]{:S(2)}, u32[]{:S(2)}) async-start(bf16[64,8,1440]{2,1,0:T(8,128)(2,1)} %bitcast.2), calls=%async_computation.1 | async-start | bytes 3145728 | tf_op jit(solution)/shard_map/all_to_all | solution.py:101
  88.6 1.2 copy-start.1
  91.2 78.9 %all-to-all-start.2 = ((bf16[64,2,2560]{2,1,0:T(2,128)(2,1)}), bf16[64,2,2560]{2,1,0:T(2,128)(2,1)S(1)}, u32[]{:S(2)}, u32[]{:S(2)}) async-start(bf16[64,2,2560]{2,1,0:T(2,128)(2,1)} %reshape.90), calls=%async_computation.2 | async-start | bytes 1310720 | tf_op jit(solution)/shard_map/all_to_all | solution.py:101
  99.7 81.6 %copy-start.8 = (f32[128,2]{0,1:T(2,128)S(1)}, f32[128,2]{0,1:T(2,128)}, u32[]{:S(2)}) copy-start(f32[128,2]{0,1:T(2,128)} %param.20) | copy-start | bytes 3076
  170.1 54.9 %all-to-all-start.3 = ((bf16[64,8,1440]{2,1,0:T(8,128)(2,1)}), bf16[64,8,1440]{2,1,0:T(8,128)(2,1)S(1)}, u32[]{:S(2)}, u32[]{:S(2)}) async-start(bf16[64,8,1440]{2,1,0:T(8,128)(2,1)} %bitcast.54), calls=%async_computation.3 | async-start | bytes 3145728 | tf_op jit(solution)/shard_map/all_to_all | solution.py:101
  184.9 35.1 %collective-permute-start = (bf16[128,512]{0,1:T(8,128)(2,1)}, bf16[128,512]{0,1:T(8,128)(2,1)}, u32[]{:S(2)}, u32[]{:S(2)}) collective-permute-start(bf16[128,512]{0,1:T(8,128)(2,1)} %copy.61), channel_id=1, source_target_pairs={{0,1},{1,2},{2,3},{3,4},{4,5},{5,6},{6,7},{7,8},{8,9},{9,10},{10,1... | collective-permute-start | bytes 393224 | tf_op jit(solution)/shard_map/ppermute | solution.py:26
  222.8 2.2 copy-start.2
  222.8 2.2 copy-start.3
Sparse Core Ops, SparseCore 0:
  11.6 142.5 all-gather.3
where the time goes:
time: 234 us; the launch traced here: 233 us
  waiting for transfers between devices  134 us (57%)
  starting transfers between devices  42.4 us (18%)
  local copies, waits for them, and re-layouts  17.3 us (7%)
  Pallas kernels  15.9 us (7%)
  between operations  14.4 us (6%)
  other arithmetic  5.53 us (2%)
  matrix products  4.12 us (2%)
    all_gather x1, waiting for transfers between devices, per_device(): lax.all_gather(jnp.concatenate([gate_block, up_block, down_block], 1), 'c...  54.5 us
    all_to_all x4, waiting for transfers between devices, exchange(): lax.all_to_all(parts, 'exp', split_axis=0, concat_axis=0, tiled=True)  49.9 us
    all_to_all x4, starting transfers between devices, exchange(): lax.all_to_all(parts, 'exp', split_axis=0, concat_axis=0, tiled=True)  40.3 us
    ppermute x1, waiting for transfers between devices, shifted(): return lax.ppermute(block, axis, route)  29.4 us
    pallas_call x1, Pallas kernels, experts_call(): pl.pallas_call(experts_kernel, out_shape=jax.ShapeDtypeStruct((slots, wid...  15.9 us
  transfers between devices with their start and end apart: 6, of which 4 were waited for; matrix products, arithmetic and copies ran while one was open for 9% of the time, Pallas kernels for 7%

commit v1 on v0

--- a/solution.py
+++ b/solution.py
@@ -16,7 +16,8 @@
 ROUTES = 2
 CAP = 8
 LANES = 128
-PANEL = 512
+WIDE = 256
+GROUPS = ((0, 4), (4, 8), (8, 11))
 VMEM_BYTES = 60 * 1024 * 1024
 
 
@@ -30,50 +31,109 @@
     return jnp.dot(choice, rows, preferred_element_type=jnp.float32).astype(jnp.bfloat16)
 
 
-def panels(width):
-    return [(low, min(low + PANEL, width)) for low in range(0, width, PANEL)]
-
-
-def experts_kernel(rows_ref, wide_ref, out_ref, sliced, wide, total, hidden, arrival):
-    count, depth = wide_ref.shape[0], wide_ref.shape[1]
-    width = rows_ref.shape[1]
-    copies = [
-        pltpu.make_async_copy(wide_ref.at[s], wide.at[s], arrival.at[s]) for s in range(count)
-    ]
-    for copy in copies:
-        copy.start()
+def pack_kernel(gate_ref, up_ref, down_ref, packed_ref):
+    depth, width = gate_ref.shape
+    main = width // LANES * LANES
+    left = width - main
+    for place, ref in enumerate((gate_ref, up_ref, down_ref)):
+        packed_ref[:, place * main : (place + 1) * main] = ref[:, :main]
+        start = 3 * main + place * left
+        packed_ref[:, start : start + left] = ref[:, main:]
+    packed_ref[:, 3 * width :] = jnp.zeros((depth, packed_ref.shape[1] - 3 * width), jnp.bfloat16)
+
+
+def pack_call(gate_block, up_block, down_block):
+    depth, width = gate_block.shape
+    packed = 3 * (width // LANES) * LANES + LANES
+    return pl.pallas_call(
+        pack_kernel,
+        out_shape=jax.ShapeDtypeStruct((depth, packed), jnp.bfloat16),
+        cost_estimate=pl.CostEstimate(
+            flops=0, bytes_accessed=12 * depth * width, transcendentals=0
+        ),
+    )(gate_block, up_block, down_block)
+
+
+def slice_kernel(rows_ref, sliced_ref):
+    count, _, depth = sliced_ref.shape
     for s in range(count):
-        sliced[s] = rows_ref[:, s * depth : (s + 1) * depth]
+        sliced_ref[s] = rows_ref[:, s * depth : (s + 1) * depth]
+
+
+def slice_call(rows, count):
+    slots, width = rows.shape
+    return pl.pallas_call(
+        slice_kernel,
+        out_shape=jax.ShapeDtypeStruct((count, slots, width // count), jnp.bfloat16),
+        cost_estimate=pl.CostEstimate(
+            flops=0, bytes_accessed=4 * slots * width, transcendentals=0
+        ),
+    )(rows)
+
+
+def experts_kernel(sliced_ref, wide_ref, out_ref, wide, hidden, resliced, arrival):
+    count, depth, packed = wide_ref.shape
+    slots, width = out_ref.shape
+    main = width // LANES * LANES
+    left = width - main
+    pieces = []
+    for low, high in GROUPS:
+        pieces.append((low * LANES, high * LANES))
+        pieces.append((main + low * LANES, main + high * LANES))
+    pieces.append((2 * main, packed))
+    copies = []
+    for place, (low, high) in enumerate(pieces):
+        piece = (slice(None), slice(None), pl.ds(low, high - low))
+        copies.append(
+            pltpu.make_async_copy(wide_ref.at[piece], wide.at[piece], arrival.at[place])
+        )
+        copies[-1].start()
+
+    def summed(left_ref, columns):
+        total = jnp.zeros((slots, WIDE), jnp.float32)
+        for s in range(count):
+            total += jnp.dot(left_ref[s], columns(s), preferred_element_type=jnp.float32)
+        return total
+
+    def hidden_tile(tile, carry):
+        low = pl.multiple_of(tile * LANES, LANES)
+        high = pl.multiple_of(main + tile * LANES, LANES)
+        both = summed(
+            sliced_ref,
+            lambda s: jnp.concatenate(
+                [wide[s, :, pl.ds(low, LANES)], wide[s, :, pl.ds(high, LANES)]], 1
+            ),
+        )
+        hidden[:, pl.ds(low, LANES)] = gated_hidden(both[:, :LANES], both[:, LANES:])
+        return carry
+
+    for group, (low, high) in enumerate(GROUPS):
+        copies[2 * group].wait()
+        copies[2 * group + 1].wait()
+        lax.fori_loop(low, high, hidden_tile, 0)
+    copies[-1].wait()
+    rest = summed(sliced_ref, lambda s: wide[s, :, packed - WIDE :])[:, LANES:]
+    hidden[:, main:] = gated_hidden(rest[:, :left], rest[:, left : 2 * left])
     for s in range(count):
-        copies[s].wait()
-        for low, high in panels(total.shape[1]):
-            part = jnp.dot(sliced[s], wide[s, :, low:high], preferred_element_type=jnp.float32)
-            total[:, low:high] = part if s == 0 else total[:, low:high] + part
-    for low, high in panels(width):
-        hidden[:, low:high] = gated_hidden(
-            total[:, low:high], total[:, width + low : width + high]
-        )
-    for s in range(count):
-        sliced[s] = hidden[:, s * depth : (s + 1) * depth]
-    start = 2 * width // LANES * LANES
-    for low, high in panels(3 * width - start):
-        part = jnp.dot(
-            sliced[0], wide[0, :, start + low : start + high], preferred_element_type=jnp.float32
-        )
-        for s in range(1, count):
-            part += jnp.dot(
-                sliced[s],
-                wide[s, :, start + low : start + high],
-                preferred_element_type=jnp.float32,
-            )
-        total[:, low:high] = part
-    lead = 2 * width - start
-    out_ref[...] = total[:, lead : lead + width].astype(jnp.bfloat16)
-
-
-def experts_call(rows, wide_all):
-    count, depth, _ = wide_all.shape
-    slots, width = rows.shape
+        resliced[s] = hidden[:, s * depth : (s + 1) * depth]
+
+    def output_tiles(place, carry):
+        low = pl.multiple_of(place * WIDE, WIDE)
+        source = pl.multiple_of(2 * main + place * WIDE, LANES)
+        total = summed(resliced, lambda s: wide[s, :, pl.ds(source, WIDE)])
+        out_ref[:, pl.ds(low, WIDE)] = total.astype(jnp.bfloat16)
+        return carry
+
+    whole = main // WIDE
+    lax.fori_loop(0, whole, output_tiles, 0)
+    last = summed(resliced, lambda s: wide[s, :, packed - WIDE :]).astype(jnp.bfloat16)
+    out_ref[:, whole * WIDE : main] = last[:, :LANES]
+    out_ref[:, main:] = last[:, LANES + 2 * left : LANES + 3 * left]
+
+
+def experts_call(sliced, wide_all):
+    count, slots, depth = sliced.shape
+    width = count * depth
     whole = pl.BlockSpec(memory_space=pltpu.VMEM)
     return pl.pallas_call(
         experts_kernel,
@@ -81,11 +141,10 @@
         in_specs=[whole, pl.BlockSpec(memory_space=pltpu.HBM)],
         out_specs=whole,
         scratch_shapes=[
+            pltpu.VMEM(wide_all.shape, jnp.bfloat16),
+            pltpu.VMEM((slots, width), jnp.bfloat16),
             pltpu.VMEM((count, slots, depth), jnp.bfloat16),
-            pltpu.VMEM(wide_all.shape, jnp.bfloat16),
-            pltpu.VMEM((slots, -(-2 * width // LANES) * LANES), jnp.float32),
-            pltpu.VMEM((slots, width), jnp.bfloat16),
-            pltpu.SemaphoreType.DMA((count,)),
+            pltpu.SemaphoreType.DMA((2 * len(GROUPS) + 1,)),
         ],
         compiler_params=pltpu.CompilerParams(vmem_limit_bytes=VMEM_BYTES),
         cost_estimate=pl.CostEstimate(
@@ -93,7 +152,7 @@
             bytes_accessed=6 * width * width + 4 * slots * width,
             transcendentals=slots * width,
         ),
-    )(rows, wide_all)
+    )(sliced, wide_all)
 
 
 def exchange(rows, peer_count):
@@ -151,9 +210,7 @@
     per_peer = tokens_here // peer_count
     gate_block, up_block, down_block = gate_w[0], up_w[0], down_w[0]
 
-    wide_all = lax.all_gather(
-        jnp.concatenate([gate_block, up_block, down_block], 1), "ctx", axis=0
-    )
+    wide_all = lax.all_gather(pack_call(gate_block, up_block, down_block), "ctx", axis=0)
 
     slot = learner_row % (peer_count * tokens_here) // tokens_here * per_peer + learner_row % per_peer
     order = (jnp.arange(tokens_here, dtype=jnp.int32)[:, None] == slot[None, :]).astype(jnp.bfloat16)
@@ -177,6 +234,7 @@
     expert_rows = exchange(outgoing, peer_count)
     packed = jnp.concatenate([queries, keys, values], 1)
     expert_rows, packed = lax.optimization_barrier((expert_rows, packed))
+    sliced = slice_call(expert_rows, lax.axis_size("ctx"))
     arrived = exchange(pick_rows(order, packed), peer_count)
     query_rows = arrived[:, : QHEADS * HEAD]
     key_value_rows = arrived[:, QHEADS * HEAD :]
@@ -193,7 +251,7 @@
 
     attn_rows = attend(query_rows, key_value_rows, sinks)
 
-    expert_out = experts_call(expert_rows, wide_all)
+    expert_out = experts_call(sliced, wide_all)
     returned = exchange(expert_out, peer_count)
     both = jnp.dot(combine, returned, preferred_element_type=jnp.float32)
     total = both[:tokens_here] + both[tokens_here:]

time: 234 us -> 235 us (level)
  Pallas kernels: 15.9 us -> 24 us
  waiting for transfers between devices: 134 us -> 129 us
  local copies, waits for them, and re-layouts: 17.3 us -> 13.5 us
    pallas_call x0 -> x2, Pallas kernels: none -> 6.24 us  [the longest x1 3.46 us: slice_call(): pl.pallas_call(slice_kernel, out_shape=jax.ShapeDtypeStruct((count, slots...]
    all_gather x1, waiting for transfers between devices: 54.5 us -> 49.6 us  [per_device(): lax.all_gather(pack_call(gate_block, up_block, down_block), 'ctx', axis=0)]
    concatenate x1 -> x0, local copies, waits for them, and re-layouts: 4.19 us -> none  [per_device(): jnp.concatenate([gate_block, up_block, down_block], 1)]
  transfers between devices with their start and end apart: 6 -> 6, of which waited for: 4 -> 4; matrix products, arithmetic and copies ran while one was open for 9% -> 10% of each run, Pallas kernels for 7% -> 9%
where the time goes in v1:
time: 235 us; the launch traced here: 234 us
  waiting for transfers between devices  129 us (55%)
  starting transfers between devices  42.4 us (18%)
  Pallas kernels  24 us (10%)
  between operations  14.4 us (6%)
  local copies, waits for them, and re-layouts  13.5 us (6%)
  other arithmetic  5.53 us (2%)
  matrix products  5.24 us (2%)
    all_to_all x4, waiting for transfers between devices, exchange(): lax.all_to_all(parts, 'exp', split_axis=0, concat_axis=0, tiled=True)  49.9 us
    all_gather x1, waiting for transfers between devices, per_device(): lax.all_gather(pack_call(gate_block, up_block, down_block), 'ctx', axis=0)  49.6 us
    all_to_all x4, starting transfers between devices, exchange(): lax.all_to_all(parts, 'exp', split_axis=0, concat_axis=0, tiled=True)  40.3 us
    ppermute x1, waiting for transfers between devices, shifted(): return lax.ppermute(block, axis, route)  29.4 us
    pallas_call x1, Pallas kernels, experts_call(): pl.pallas_call(experts_kernel, out_shape=jax.ShapeDtypeStruct((slots, wid...  17.8 us
  transfers between devices with their start and end apart: 6, of which 4 were waited for; matrix products, arithmetic and copies ran while one was open for 10% of the time, Pallas kernels for 9%

profile of v1, /device:TPU:6, one launch (start us, length us, event | category | flops | bytes accessed | tf_op | source)
XLA Modules:
  0.0 233.9 jit_solution(17189233149722132413)
XLA Ops:
  7.2 2.8 %shard_map.132 = bf16[180,4352]{1,0:T(8,128)(2,1)} custom-call(bf16[180,1440]{1,0:T(8,128)(2,1)} %bitcast.57, bf16[180,1440]{1,0:T(8,128)(2,1)} %bitcast.58, bf16[180,1440]{1,0:T(8,128)(2,1)} %bitcast.59), custom_call_target="tpu_custom_call" | custom-call | bytes 3110400 | tf_op jit(solution)/shard_map/pallas_call | solution.py:48
  10.6 0.9 reshape.87
  11.5 14.0 %all-to-all-start = ((bf16[64,2,1440]{2,1,0:T(2,128)(2,1)}), bf16[64,2,1440]{2,1,0:T(2,128)(2,1)S(1)}, u32[]{:S(2)}, u32[]{:S(2)}) async-start(bf16[64,2,1440]{2,1,0:T(2,128)(2,1)} %reshape.87), calls=%async_computation | async-start | bytes 786432 | tf_op jit(solution)/shard_map/all_to_all | solution.py:160
  26.2 13.4 %all-to-all-done = bf16[64,2,1440]{2,1,0:T(2,128)(2,1)S(1)} async-done(((bf16[64,2,1440]{2,1,0:T(2,128)(2,1)}), bf16[64,2,1440]{2,1,0:T(2,128)(2,1)S(1)}, u32[]{:S(2)}, u32[]{:S(2)}) %all-to-all-start) | async-done | bytes 368672 | tf_op jit(solution)/shard_map/all_to_all | solution.py:160
  39.6 0.5 multiply_reduce_fusion
  40.5 0.7 convolution_convert_fusion.1
  41.2 1.6 copy.52
  42.8 6.8 %all-to-all-start.1 = ((bf16[64,8,1440]{2,1,0:T(8,128)(2,1)}), bf16[64,8,1440]{2,1,0:T(8,128)(2,1)S(1)}, u32[]{:S(2)}, u32[]{:S(2)}) async-start(bf16[64,8,1440]{2,1,0:T(8,128)(2,1)} %bitcast.54), calls=%async_computation.1 | async-start | bytes 3145728 | tf_op jit(solution)/shard_map/all_to_all | solution.py:160
  49.6 1.1 pad_maximum_fusion
  50.7 36.5 %all-to-all-done.1 = bf16[64,8,1440]{2,1,0:T(8,128)(2,1)S(1)} async-done(((bf16[64,8,1440]{2,1,0:T(8,128)(2,1)}), bf16[64,8,1440]{2,1,0:T(8,128)(2,1)S(1)}, u32[]{:S(2)}, u32[]{:S(2)}) %all-to-all-start.1) | async-done | bytes 1474592 | tf_op jit(solution)/shard_map/all_to_all | solution.py:160
  87.2 1.4 convolution_convert_fusion
  88.6 2.6 %reshape.90 = bf16[64,2,2560]{2,1,0:T(2,128)(2,1)} reshape(bf16[128,2560]{1,0:T(8,128)(2,1)} %convolution_convert_fusion) | data formatting | bytes 1310720 | tf_op jit(solution)/shard_map/reshape | solution.py:159
  91.2 8.3 %all-to-all-start.2 = ((bf16[64,2,2560]{2,1,0:T(2,128)(2,1)}), bf16[64,2,2560]{2,1,0:T(2,128)(2,1)S(1)}, u32[]{:S(2)}, u32[]{:S(2)}) async-start(bf16[64,2,2560]{2,1,0:T(2,128)(2,1)} %reshape.90), calls=%async_computation.2 | async-start | bytes 1310720 | tf_op jit(solution)/shard_map/all_to_all | solution.py:160
  99.7 3.5 %shard_map.131.sliced_ref = bf16[8,512,180]{2,1,0:T(8,128)(2,1)} custom-call(bf16[512,1440]{1,0:T(8,128)(2,1)} %bitcast.53), custom_call_target="tpu_custom_call" | custom-call | bytes 2949120 | tf_op jit(solution)/shard_map/pallas_call | solution.py:65
  103.2 49.6 %all-gather.4.cloned.1.call-done.wide_ref = bf16[8,180,4352]{2,1,0:T(8,128)(2,1)} async-done(((bf16[1,180,4352]{2,1,0:T(8,128)(2,1)}), bf16[8,180,4352]{2,1,0:T(8,128)(2,1)}) %all-gather.4.cloned.1.call-update) | async-done | bytes 12533776 | tf_op jit(solution)/shard_map/all_gather | solution.py:213
  152.7 17.8 %shard_map.133 = bf16[512,1440]{1,0:T(8,128)(2,1)} custom-call(bf16[8,512,180]{2,1,0:T(8,128)(2,1)} %shard_map.131.sliced_ref, bf16[8,180,4352]{2,1,0:T(8,128)(2,1)} %all-gather.4.cloned.1.call-done.wide_ref), custom_call_target="tpu_custom_call" | custom-call | flops 6370099200 | bytes 15390720 | tf_op jit(solution)/shard_map/pallas_call | solution.py:138
  170.5 11.1 %all-to-all-start.3 = ((bf16[64,8,1440]{2,1,0:T(8,128)(2,1)}), bf16[64,8,1440]{2,1,0:T(8,128)(2,1)S(1)}, u32[]{:S(2)}, u32[]{:S(2)}) async-start(bf16[64,8,1440]{2,1,0:T(8,128)(2,1)} %bitcast.56), calls=%async_computation.3 | async-start | bytes 3145728 | tf_op jit(solution)/shard_map/all_to_all | solution.py:160
  181.7 0.9 add_convert_fusion.1
  182.5 1.1 reshape.91
  183.6 0.9 slice.52
  184.5 0.8 copy.61
  185.3 2.0 collective-permute-start
  187.8 1.9 slice.55
  189.6 1.3 copy.62
  191.0 29.4 %collective-permute-done = bf16[128,512]{0,1:T(8,128)(2,1)} collective-permute-done((bf16[128,512]{0,1:T(8,128)(2,1)}, bf16[128,512]{0,1:T(8,128)(2,1)}, u32[]{:S(2)}, u32[]{:S(2)}) %collective-permute-start) | collective-permute-done | bytes 131104 | tf_op jit(solution)/shard_map/ppermute | solution.py:27
  220.4 1.0 pad_maximum_fusion.1
  221.3 0.8 fusion.1
  222.2 0.9 fusion
  223.2 1.2 fusion.5
  224.3 1.0 copy.57
  225.4 0.8 fusion.3
  226.2 0.9 fusion.8
  (50 shorter events, 2.3 us)
Async XLA Ops:
  7.2 2.9 %copy-start = (bf16[128,1440]{0,1:T(8,128)(2,1)S(1)}, bf16[128,1440]{0,1:T(8,128)(2,1)}, u32[]{:S(2)}) copy-start(bf16[128,1440]{0,1:T(8,128)(2,1)} %param.12) | copy-start | bytes 1105924
  7.2 2.9 %copy-start.10 = (s32[128]{0:T(128)S(1)}, s32[128]{0:T(128)}, u32[]{:S(2)}) copy-start(s32[128]{0:T(128)} %param.18) | copy-start | bytes 1540
  7.2 18.3 %copy-start.7 = (s32[128,2]{0,1:T(2,128)S(1)}, s32[128,2]{0,1:T(2,128)}, u32[]{:S(2)}) copy-start(s32[128,2]{0,1:T(2,128)} %param.19) | copy-start | bytes 3076
  7.2 145.5 %all-gather.4.cloned.1.call-start = ((), (), s32[]{:S(2)}) async-start(), calls=%async_computation.4 | async-start | bytes 14413824 | tf_op jit(solution)/shard_map/all_gather | solution.py:213
  10.0 30.5 %copy-start.6 = (f32[1440]{0:T(1024)S(1)}, f32[1440]{0:T(1024)}, u32[]{:S(2)}) copy-start(f32[1440]{0:T(1024)} %param.17) | copy-start | bytes 17284
  11.5 28.2 %all-to-all-start = ((bf16[64,2,1440]{2,1,0:T(2,128)(2,1)}), bf16[64,2,1440]{2,1,0:T(2,128)(2,1)S(1)}, u32[]{:S(2)}, u32[]{:S(2)}) async-start(bf16[64,2,1440]{2,1,0:T(2,128)(2,1)} %reshape.87), calls=%async_computation | async-start | bytes 786432 | tf_op jit(solution)/shard_map/all_to_all | solution.py:160
  40.5 9.1 %copy-start.4 = (bf16[128,256]{1,0:T(8,128)(2,1)S(1)}, bf16[128,256]{1,0:T(8,128)(2,1)}, u32[]{:S(2)}) copy-start(bf16[128,256]{1,0:T(8,128)(2,1)} %param.15) | copy-start | bytes 196612
  40.5 9.1 %copy-start.5 = (bf16[128,256]{1,0:T(8,128)(2,1)S(1)}, bf16[128,256]{1,0:T(8,128)(2,1)}, u32[]{:S(2)}) copy-start(bf16[128,256]{1,0:T(8,128)(2,1)} %param.14) | copy-start | bytes 196612
  42.8 56.8 %copy-start.9 = (f32[32]{0:T(128)S(1)}, f32[32]{0:T(128)}, u32[]{:S(2)}) copy-start(f32[32]{0:T(128)} %param.16) | copy-start | bytes 388
  42.8 44.4 %all-to-all-start.1 = ((bf16[64,8,1440]{2,1,0:T(8,128)(2,1)}), bf16[64,8,1440]{2,1,0:T(8,128)(2,1)S(1)}, u32[]{:S(2)}, u32[]{:S(2)}) async-start(bf16[64,8,1440]{2,1,0:T(8,128)(2,1)} %bitcast.54), calls=%async_computation.1 | async-start | bytes 3145728 | tf_op jit(solution)/shard_map/all_to_all | solution.py:160
  87.2 12.5 %copy-start.1 = (bf16[64,8,1440]{2,1,0:T(8,128)(2,1)}, bf16[64,8,1440]{2,1,0:T(8,128)(2,1)S(1)}, u32[]{:S(2)}) copy-start(bf16[64,8,1440]{2,1,0:T(8,128)(2,1)S(1)} %all-to-all-done.1) | copy-start | bytes 4423684
  91.2 79.3 %all-to-all-start.2 = ((bf16[64,2,2560]{2,1,0:T(2,128)(2,1)}), bf16[64,2,2560]{2,1,0:T(2,128)(2,1)S(1)}, u32[]{:S(2)}, u32[]{:S(2)}) async-start(bf16[64,2,2560]{2,1,0:T(2,128)(2,1)} %reshape.90), calls=%async_computation.2 | async-start | bytes 1310720 | tf_op jit(solution)/shard_map/all_to_all | solution.py:160
  103.2 78.5 %copy-start.8 = (f32[128,2]{0,1:T(2,128)S(1)}, f32[128,2]{0,1:T(2,128)}, u32[]{:S(2)}) copy-start(f32[128,2]{0,1:T(2,128)} %param.20) | copy-start | bytes 3076
  170.5 54.9 %all-to-all-start.3 = ((bf16[64,8,1440]{2,1,0:T(8,128)(2,1)}), bf16[64,8,1440]{2,1,0:T(8,128)(2,1)S(1)}, u32[]{:S(2)}, u32[]{:S(2)}) async-start(bf16[64,8,1440]{2,1,0:T(8,128)(2,1)} %bitcast.56), calls=%async_computation.3 | async-start | bytes 3145728 | tf_op jit(solution)/shard_map/all_to_all | solution.py:160
  185.3 35.1 %collective-permute-start = (bf16[128,512]{0,1:T(8,128)(2,1)}, bf16[128,512]{0,1:T(8,128)(2,1)}, u32[]{:S(2)}, u32[]{:S(2)}) collective-permute-start(bf16[128,512]{0,1:T(8,128)(2,1)} %copy.61), channel_id=1, source_target_pairs={{0,1},{1,2},{2,3},{3,4},{4,5},{5,6},{6,7},{7,8},{8,9},{9,10},{10,1... | collective-permute-start | bytes 393224 | tf_op jit(solution)/shard_map/ppermute | solution.py:27
  223.2 2.2 copy-start.2
  223.2 2.2 copy-start.3
Sparse Core Ops, SparseCore 0:
  10.2 142.5 all-gather.3

commit v2 on v1

--- a/solution.py
+++ b/solution.py
@@ -16,8 +16,8 @@
 ROUTES = 2
 CAP = 8
 LANES = 128
-WIDE = 256
-GROUPS = ((0, 4), (4, 8), (8, 11))
+ROWS = 8
+GROUPS = ((0, 2), (2, 4), (4, 5))
 VMEM_BYTES = 60 * 1024 * 1024
 
 
@@ -31,15 +31,21 @@
     return jnp.dot(choice, rows, preferred_element_type=jnp.float32).astype(jnp.bfloat16)
 
 
+def pitch_of(depth):
+    return -(-depth // ROWS) * ROWS
+
+
 def pack_kernel(gate_ref, up_ref, down_ref, packed_ref):
     depth, width = gate_ref.shape
     main = width // LANES * LANES
     left = width - main
+    pitch, packed = packed_ref.shape
+    packed_ref[depth:, :] = jnp.zeros((pitch - depth, packed), jnp.bfloat16)
     for place, ref in enumerate((gate_ref, up_ref, down_ref)):
-        packed_ref[:, place * main : (place + 1) * main] = ref[:, :main]
+        packed_ref[:depth, place * main : (place + 1) * main] = ref[:, :main]
         start = 3 * main + place * left
-        packed_ref[:, start : start + left] = ref[:, main:]
-    packed_ref[:, 3 * width :] = jnp.zeros((depth, packed_ref.shape[1] - 3 * width), jnp.bfloat16)
+        packed_ref[:depth, start : start + left] = ref[:, main:]
+    packed_ref[:depth, 3 * width :] = jnp.zeros((depth, packed - 3 * width), jnp.bfloat16)
 
 
 def pack_call(gate_block, up_block, down_block):
@@ -47,104 +53,120 @@
     packed = 3 * (width // LANES) * LANES + LANES
     return pl.pallas_call(
         pack_kernel,
-        out_shape=jax.ShapeDtypeStruct((depth, packed), jnp.bfloat16),
+        out_shape=jax.ShapeDtypeStruct((pitch_of(depth), packed), jnp.bfloat16),
         cost_estimate=pl.CostEstimate(
             flops=0, bytes_accessed=12 * depth * width, transcendentals=0
         ),
     )(gate_block, up_block, down_block)
 
 
-def slice_kernel(rows_ref, sliced_ref):
-    count, _, depth = sliced_ref.shape
-    for s in range(count):
-        sliced_ref[s] = rows_ref[:, s * depth : (s + 1) * depth]
-
-
-def slice_call(rows, count):
+def spread(source, target, depth):
+    pitch = pitch_of(depth)
+    for s in range(source.shape[1] // depth):
+        target[:, s * pitch : s * pitch + depth] = source[:, s * depth : (s + 1) * depth]
+        target[:, s * pitch + depth : (s + 1) * pitch] = jnp.zeros(
+            (source.shape[0], pitch - depth), jnp.bfloat16
+        )
+
+
+def spread_call(rows, depth):
     slots, width = rows.shape
+
+    def spread_kernel(rows_ref, spread_ref):
+        spread(rows_ref, spread_ref, depth)
+
     return pl.pallas_call(
-        slice_kernel,
-        out_shape=jax.ShapeDtypeStruct((count, slots, width // count), jnp.bfloat16),
+        spread_kernel,
+        out_shape=jax.ShapeDtypeStruct((slots, width // depth * pitch_of(depth)), jnp.bfloat16),
         cost_estimate=pl.CostEstimate(
             flops=0, bytes_accessed=4 * slots * width, transcendentals=0
         ),
     )(rows)
 
 
-def experts_kernel(sliced_ref, wide_ref, out_ref, wide, hidden, resliced, arrival):
-    count, depth, packed = wide_ref.shape
-    slots, width = out_ref.shape
+def experts_kernel(depth, rows_ref, wide_ref, out_ref, wide, hidden, again, arrival):
+    packed = wide_ref.shape[1]
+    width = out_ref.shape[1]
     main = width // LANES * LANES
     left = width - main
+    step = 2 * LANES
     pieces = []
     for low, high in GROUPS:
-        pieces.append((low * LANES, high * LANES))
-        pieces.append((main + low * LANES, main + high * LANES))
-    pieces.append((2 * main, packed))
+        pieces.append((low * step, high * step))
+        pieces.append((main + low * step, main + high * step))
+    done = GROUPS[-1][1] * step
+    pieces += [(done, main), (main + done, packed)]
     copies = []
     for place, (low, high) in enumerate(pieces):
-        piece = (slice(None), slice(None), pl.ds(low, high - low))
+        piece = (slice(None), pl.ds(low, high - low))
         copies.append(
             pltpu.make_async_copy(wide_ref.at[piece], wide.at[piece], arrival.at[place])
         )
         copies[-1].start()
 
-    def summed(left_ref, columns):
-        total = jnp.zeros((slots, WIDE), jnp.float32)
-        for s in range(count):
-            total += jnp.dot(left_ref[s], columns(s), preferred_element_type=jnp.float32)
-        return total
-
-    def hidden_tile(tile, carry):
-        low = pl.multiple_of(tile * LANES, LANES)
-        high = pl.multiple_of(main + tile * LANES, LANES)
-        both = summed(
-            sliced_ref,
-            lambda s: jnp.concatenate(
-                [wide[s, :, pl.ds(low, LANES)], wide[s, :, pl.ds(high, LANES)]], 1
-            ),
+    def product(left_ref, columns):
+        return jnp.dot(left_ref[...], columns, preferred_element_type=jnp.float32)
+
+    def hidden_tiles(place, carry):
+        low = pl.multiple_of(place * step, step)
+        high = pl.multiple_of(main + place * step, LANES)
+        both = product(
+            rows_ref, jnp.concatenate([wide[:, pl.ds(low, step)], wide[:, pl.ds(high, step)]], 1)
         )
-        hidden[:, pl.ds(low, LANES)] = gated_hidden(both[:, :LANES], both[:, LANES:])
+        hidden[:, pl.ds(low, step)] = gated_hidden(both[:, :step], both[:, step:])
         return carry
 
     for group, (low, high) in enumerate(GROUPS):
         copies[2 * group].wait()
         copies[2 * group + 1].wait()
-        lax.fori_loop(low, high, hidden_tile, 0)
+        lax.fori_loop(low, high, hidden_tiles, 0)
+    copies[-2].wait()
     copies[-1].wait()
-    rest = summed(sliced_ref, lambda s: wide[s, :, packed - WIDE :])[:, LANES:]
+    both = product(
+        rows_ref,
+        jnp.concatenate(
+            [wide[:, done:main], wide[:, main + done : 2 * main], wide[:, 3 * main :]], 1
+        ),
+    )
+    span = main - done
+    rest = both[:, 2 * span :]
+    hidden[:, done:main] = gated_hidden(both[:, :span], both[:, span : 2 * span])
     hidden[:, main:] = gated_hidden(rest[:, :left], rest[:, left : 2 * left])
-    for s in range(count):
-        resliced[s] = hidden[:, s * depth : (s + 1) * depth]
+    spread(hidden, again, depth)
 
     def output_tiles(place, carry):
-        low = pl.multiple_of(place * WIDE, WIDE)
-        source = pl.multiple_of(2 * main + place * WIDE, LANES)
-        total = summed(resliced, lambda s: wide[s, :, pl.ds(source, WIDE)])
-        out_ref[:, pl.ds(low, WIDE)] = total.astype(jnp.bfloat16)
+        low = pl.multiple_of(place * 2 * step, 2 * step)
+        source = pl.multiple_of(2 * main + place * 2 * step, LANES)
+        total = product(again, wide[:, pl.ds(source, 2 * step)])
+        out_ref[:, pl.ds(low, 2 * step)] = total.astype(jnp.bfloat16)
         return carry
 
-    whole = main // WIDE
+    whole = main // (2 * step)
     lax.fori_loop(0, whole, output_tiles, 0)
-    last = summed(resliced, lambda s: wide[s, :, packed - WIDE :]).astype(jnp.bfloat16)
-    out_ref[:, whole * WIDE : main] = last[:, :LANES]
-    out_ref[:, main:] = last[:, LANES + 2 * left : LANES + 3 * left]
-
-
-def experts_call(sliced, wide_all):
-    count, slots, depth = sliced.shape
-    width = count * depth
+    first = whole * 2 * step
+    last = product(again, wide[:, 2 * main + first :]).astype(jnp.bfloat16)
+    out_ref[:, first:main] = last[:, : main - first]
+    tail = main - first + 2 * left
+    out_ref[:, main:] = last[:, tail : tail + left]
+
+
+def experts_call(rows, wide_all, depth, width):
+    slots = rows.shape[0]
     whole = pl.BlockSpec(memory_space=pltpu.VMEM)
+
+    def kernel(*refs):
+        experts_kernel(depth, *refs)
+
     return pl.pallas_call(
-        experts_kernel,
+        kernel,
         out_shape=jax.ShapeDtypeStruct((slots, width), jnp.bfloat16),
         in_specs=[whole, pl.BlockSpec(memory_space=pltpu.HBM)],
         out_specs=whole,
         scratch_shapes=[
             pltpu.VMEM(wide_all.shape, jnp.bfloat16),
             pltpu.VMEM((slots, width), jnp.bfloat16),
-            pltpu.VMEM((count, slots, depth), jnp.bfloat16),
-            pltpu.SemaphoreType.DMA((2 * len(GROUPS) + 1,)),
+            pltpu.VMEM(rows.shape, jnp.bfloat16),
+            pltpu.SemaphoreType.DMA((2 * len(GROUPS) + 2,)),
         ],
         compiler_params=pltpu.CompilerParams(vmem_limit_bytes=VMEM_BYTES),
         cost_estimate=pl.CostEstimate(
@@ -152,7 +174,7 @@
             bytes_accessed=6 * width * width + 4 * slots * width,
             transcendentals=slots * width,
         ),
-    )(sliced, wide_all)
+    )(rows, wide_all)
 
 
 def exchange(rows, peer_count):
@@ -210,7 +232,9 @@
     per_peer = tokens_here // peer_count
     gate_block, up_block, down_block = gate_w[0], up_w[0], down_w[0]
 
-    wide_all = lax.all_gather(pack_call(gate_block, up_block, down_block), "ctx", axis=0)
+    depth, width = gate_block.shape
+    wide = pack_call(gate_block, up_block, down_block)
+    wide_all = lax.all_gather(wide, "ctx", axis=0, tiled=True)
 
     slot = learner_row % (peer_count * tokens_here) // tokens_here * per_peer + learner_row % per_peer
     order = (jnp.arange(tokens_here, dtype=jnp.int32)[:, None] == slot[None, :]).astype(jnp.bfloat16)
@@ -234,7 +258,7 @@
     expert_rows = exchange(outgoing, peer_count)
     packed = jnp.concatenate([queries, keys, values], 1)
     expert_rows, packed = lax.optimization_barrier((expert_rows, packed))
-    sliced = slice_call(expert_rows, lax.axis_size("ctx"))
+    spread_rows = spread_call(expert_rows, depth)
     arrived = exchange(pick_rows(order, packed), peer_count)
     query_rows = arrived[:, : QHEADS * HEAD]
     key_value_rows = arrived[:, QHEADS * HEAD :]
@@ -251,7 +275,7 @@
 
     attn_rows = attend(query_rows, key_value_rows, sinks)
 
-    expert_out = experts_call(sliced, wide_all)
+    expert_out = experts_call(spread_rows, wide_all, depth, width)
     returned = exchange(expert_out, peer_count)
     both = jnp.dot(combine, returned, preferred_element_type=jnp.float32)
     total = both[:tokens_here] + both[tokens_here:]

time: 235 us -> 231 us (0.983)
  Pallas kernels: 24 us -> 19.8 us
    pallas_call x3, Pallas kernels: 24 us -> 19.8 us  [the longest x1 13.7 us: experts_call(): pl.pallas_call(kernel, out_shape=jax.ShapeDtypeStruct((slots, width), jnp...]
  transfers between devices with their start and end apart: 6 -> 6, of which waited for: 4 -> 4; matrix products, arithmetic and copies ran while one was open for 10% -> 10% of each run, Pallas kernels for 9% -> 7%
where the time goes in v2:
time: 231 us; the launch traced here: 230 us
  waiting for transfers between devices  129 us (56%)
  starting transfers between devices  42.4 us (18%)
  Pallas kernels  19.8 us (9%)
  between operations  14.4 us (6%)
  local copies, waits for them, and re-layouts  13.5 us (6%)
  other arithmetic  5.53 us (2%)
  matrix products  5.15 us (2%)
    all_to_all x4, waiting for transfers between devices, exchange(): lax.all_to_all(parts, 'exp', split_axis=0, concat_axis=0, tiled=True)  49.9 us
    all_gather x1, waiting for transfers between devices, per_device(): wide_all = lax.all_gather(wide, 'ctx', axis=0, tiled=True)  49.8 us
    all_to_all x4, starting transfers between devices, exchange(): lax.all_to_all(parts, 'exp', split_axis=0, concat_axis=0, tiled=True)  40.3 us
    ppermute x1, waiting for transfers between devices, shifted(): return lax.ppermute(block, axis, route)  29.4 us
    pallas_call x1, Pallas kernels, experts_call(): pl.pallas_call(kernel, out_shape=jax.ShapeDtypeStruct((slots, width), jnp...  13.7 us
  transfers between devices with their start and end apart: 6, of which 4 were waited for; matrix products, arithmetic and copies ran while one was open for 10% of the time, Pallas kernels for 7%

profile of v2, /device:TPU:6, one launch (start us, length us, event | category | flops | bytes accessed | tf_op | source)
XLA Modules:
  0.0 229.8 jit_solution(4566328346889033021)
XLA Ops:
  7.2 2.8 %shard_map.132 = bf16[184,4352]{1,0:T(8,128)(2,1)} custom-call(bf16[180,1440]{1,0:T(8,128)(2,1)} %bitcast.55, bf16[180,1440]{1,0:T(8,128)(2,1)} %bitcast.56, bf16[180,1440]{1,0:T(8,128)(2,1)} %bitcast.57), custom_call_target="tpu_custom_call" | custom-call | bytes 3110400 | tf_op jit(solution)/shard_map/pallas_call | solution.py:54
  10.5 0.9 reshape.87
  11.4 14.0 %all-to-all-start = ((bf16[64,2,1440]{2,1,0:T(2,128)(2,1)}), bf16[64,2,1440]{2,1,0:T(2,128)(2,1)S(1)}, u32[]{:S(2)}, u32[]{:S(2)}) async-start(bf16[64,2,1440]{2,1,0:T(2,128)(2,1)} %reshape.87), calls=%async_computation | async-start | bytes 786432 | tf_op jit(solution)/shard_map/all_to_all | solution.py:182
  26.2 13.4 %all-to-all-done = bf16[64,2,1440]{2,1,0:T(2,128)(2,1)S(1)} async-done(((bf16[64,2,1440]{2,1,0:T(2,128)(2,1)}), bf16[64,2,1440]{2,1,0:T(2,128)(2,1)S(1)}, u32[]{:S(2)}, u32[]{:S(2)}) %all-to-all-start) | async-done | bytes 368672 | tf_op jit(solution)/shard_map/all_to_all | solution.py:182
  39.6 0.5 multiply_reduce_fusion
  40.5 0.7 convolution_convert_fusion.1
  41.2 1.6 copy.42
  42.8 6.8 %all-to-all-start.1 = ((bf16[64,8,1440]{2,1,0:T(8,128)(2,1)}), bf16[64,8,1440]{2,1,0:T(8,128)(2,1)S(1)}, u32[]{:S(2)}, u32[]{:S(2)}) async-start(bf16[64,8,1440]{2,1,0:T(8,128)(2,1)} %bitcast.52), calls=%async_computation.1 | async-start | bytes 3145728 | tf_op jit(solution)/shard_map/all_to_all | solution.py:182
  49.6 1.1 pad_maximum_fusion
  50.7 36.5 %all-to-all-done.1 = bf16[64,8,1440]{2,1,0:T(8,128)(2,1)S(1)} async-done(((bf16[64,8,1440]{2,1,0:T(8,128)(2,1)}), bf16[64,8,1440]{2,1,0:T(8,128)(2,1)S(1)}, u32[]{:S(2)}, u32[]{:S(2)}) %all-to-all-start.1) | async-done | bytes 1474592 | tf_op jit(solution)/shard_map/all_to_all | solution.py:182
  87.2 1.3 convolution_convert_fusion
  88.5 2.6 %reshape.90 = bf16[64,2,2560]{2,1,0:T(2,128)(2,1)} reshape(bf16[128,2560]{1,0:T(8,128)(2,1)} %convolution_convert_fusion) | data formatting | bytes 1310720 | tf_op jit(solution)/shard_map/reshape | solution.py:181
  91.2 8.4 %all-to-all-start.2 = ((bf16[64,2,2560]{2,1,0:T(2,128)(2,1)}), bf16[64,2,2560]{2,1,0:T(2,128)(2,1)S(1)}, u32[]{:S(2)}, u32[]{:S(2)}) async-start(bf16[64,2,2560]{2,1,0:T(2,128)(2,1)} %reshape.90), calls=%async_computation.2 | async-start | bytes 1310720 | tf_op jit(solution)/shard_map/all_to_all | solution.py:182
  99.7 3.3 %shard_map.131.refs_0_ = bf16[512,1472]{1,0:T(8,128)(2,1)} custom-call(bf16[512,1440]{1,0:T(8,128)(2,1)} %bitcast.51), custom_call_target="tpu_custom_call" | custom-call | bytes 2949120 | tf_op jit(solution)/shard_map/pallas_call | solution.py:78
  103.0 49.8 %all-gather.2.cloned.1.call-done.refs_1_ = bf16[1472,4352]{1,0:T(8,128)(2,1)} async-done(((bf16[184,4352]{1,0:T(8,128)(2,1)}), bf16[1472,4352]{1,0:T(8,128)(2,1)}) %all-gather.2.cloned.1.call-update) | async-done | bytes 12812304 | tf_op jit(solution)/shard_map/all_gather | solution.py:237
  152.7 13.7 %shard_map.133 = bf16[512,1440]{1,0:T(8,128)(2,1)} custom-call(bf16[512,1472]{1,0:T(8,128)(2,1)} %shard_map.131.refs_0_, bf16[1472,4352]{1,0:T(8,128)(2,1)} %all-gather.2.cloned.1.call-done.refs_1_), custom_call_target="tpu_custom_call" | custom-call | flops 6370099200 | bytes 15390720 | tf_op jit(solution)/shard_map/pallas_call | solution.py:160
  166.5 11.1 %all-to-all-start.3 = ((bf16[64,8,1440]{2,1,0:T(8,128)(2,1)}), bf16[64,8,1440]{2,1,0:T(8,128)(2,1)S(1)}, u32[]{:S(2)}, u32[]{:S(2)}) async-start(bf16[64,8,1440]{2,1,0:T(8,128)(2,1)} %bitcast.54), calls=%async_computation.3 | async-start | bytes 3145728 | tf_op jit(solution)/shard_map/all_to_all | solution.py:182
  177.6 0.9 add_convert_fusion.1
  178.5 1.1 reshape.91
  179.6 0.9 slice.52
  180.5 0.8 copy.51
  181.3 2.0 collective-permute-start
  183.7 1.9 slice.55
  185.6 1.3 copy.52
  186.9 29.4 %collective-permute-done = bf16[128,512]{0,1:T(8,128)(2,1)} collective-permute-done((bf16[128,512]{0,1:T(8,128)(2,1)}, bf16[128,512]{0,1:T(8,128)(2,1)}, u32[]{:S(2)}, u32[]{:S(2)}) %collective-permute-start) | collective-permute-done | bytes 131104 | tf_op jit(solution)/shard_map/ppermute | solution.py:27
  216.3 1.0 pad_maximum_fusion.1
  217.3 0.8 fusion.1
  218.1 0.9 fusion
  219.1 1.2 fusion.5
  220.3 1.0 copy.47
  221.3 0.8 fusion.3
  222.1 0.9 fusion.8
  (50 shorter events, 2.3 us)
Async XLA Ops:
  7.2 2.9 %copy-start = (bf16[128,1440]{0,1:T(8,128)(2,1)S(1)}, bf16[128,1440]{0,1:T(8,128)(2,1)}, u32[]{:S(2)}) copy-start(bf16[128,1440]{0,1:T(8,128)(2,1)} %param.12) | copy-start | bytes 1105924
  7.2 2.9 %copy-start.10 = (s32[128]{0:T(128)S(1)}, s32[128]{0:T(128)}, u32[]{:S(2)}) copy-start(s32[128]{0:T(128)} %param.18) | copy-start | bytes 1540
  7.2 18.3 %copy-start.7 = (s32[128,2]{0,1:T(2,128)S(1)}, s32[128,2]{0,1:T(2,128)}, u32[]{:S(2)}) copy-start(s32[128,2]{0,1:T(2,128)} %param.19) | copy-start | bytes 3076
  7.2 145.5 %all-gather.2.cloned.1.call-start = ((), (), s32[]{:S(2)}) async-start(), calls=%async_computation.4 | async-start | bytes 14413824 | tf_op jit(solution)/shard_map/all_gather | solution.py:237
  10.0 30.5 %copy-start.6 = (f32[1440]{0:T(1024)S(1)}, f32[1440]{0:T(1024)}, u32[]{:S(2)}) copy-start(f32[1440]{0:T(1024)} %param.17) | copy-start | bytes 17284
  11.4 28.2 %all-to-all-start = ((bf16[64,2,1440]{2,1,0:T(2,128)(2,1)}), bf16[64,2,1440]{2,1,0:T(2,128)(2,1)S(1)}, u32[]{:S(2)}, u32[]{:S(2)}) async-start(bf16[64,2,1440]{2,1,0:T(2,128)(2,1)} %reshape.87), calls=%async_computation | async-start | bytes 786432 | tf_op jit(solution)/shard_map/all_to_all | solution.py:182
  40.5 9.1 %copy-start.4 = (bf16[128,256]{1,0:T(8,128)(2,1)S(1)}, bf16[128,256]{1,0:T(8,128)(2,1)}, u32[]{:S(2)}) copy-start(bf16[128,256]{1,0:T(8,128)(2,1)} %param.15) | copy-start | bytes 196612
  40.5 9.1 %copy-start.5 = (bf16[128,256]{1,0:T(8,128)(2,1)S(1)}, bf16[128,256]{1,0:T(8,128)(2,1)}, u32[]{:S(2)}) copy-start(bf16[128,256]{1,0:T(8,128)(2,1)} %param.14) | copy-start | bytes 196612
  42.8 56.8 %copy-start.9 = (f32[32]{0:T(128)S(1)}, f32[32]{0:T(128)}, u32[]{:S(2)}) copy-start(f32[32]{0:T(128)} %param.16) | copy-start | bytes 388
  42.8 44.4 %all-to-all-start.1 = ((bf16[64,8,1440]{2,1,0:T(8,128)(2,1)}), bf16[64,8,1440]{2,1,0:T(8,128)(2,1)S(1)}, u32[]{:S(2)}, u32[]{:S(2)}) async-start(bf16[64,8,1440]{2,1,0:T(8,128)(2,1)} %bitcast.52), calls=%async_computation.1 | async-start | bytes 3145728 | tf_op jit(solution)/shard_map/all_to_all | solution.py:182
  87.2 12.5 %copy-start.1 = (bf16[64,8,1440]{2,1,0:T(8,128)(2,1)}, bf16[64,8,1440]{2,1,0:T(8,128)(2,1)S(1)}, u32[]{:S(2)}) copy-start(bf16[64,8,1440]{2,1,0:T(8,128)(2,1)S(1)} %all-to-all-done.1) | copy-start | bytes 4423684
  91.2 75.3 %all-to-all-start.2 = ((bf16[64,2,2560]{2,1,0:T(2,128)(2,1)}), bf16[64,2,2560]{2,1,0:T(2,128)(2,1)S(1)}, u32[]{:S(2)}, u32[]{:S(2)}) async-start(bf16[64,2,2560]{2,1,0:T(2,128)(2,1)} %reshape.90), calls=%async_computation.2 | async-start | bytes 1310720 | tf_op jit(solution)/shard_map/all_to_all | solution.py:182
  103.0 74.6 %copy-start.8 = (f32[128,2]{0,1:T(2,128)S(1)}, f32[128,2]{0,1:T(2,128)}, u32[]{:S(2)}) copy-start(f32[128,2]{0,1:T(2,128)} %param.20) | copy-start | bytes 3076
  166.5 54.9 %all-to-all-start.3 = ((bf16[64,8,1440]{2,1,0:T(8,128)(2,1)}), bf16[64,8,1440]{2,1,0:T(8,128)(2,1)S(1)}, u32[]{:S(2)}, u32[]{:S(2)}) async-start(bf16[64,8,1440]{2,1,0:T(8,128)(2,1)} %bitcast.54), calls=%async_computation.3 | async-start | bytes 3145728 | tf_op jit(solution)/shard_map/all_to_all | solution.py:182
  181.3 35.1 %collective-permute-start = (bf16[128,512]{0,1:T(8,128)(2,1)}, bf16[128,512]{0,1:T(8,128)(2,1)}, u32[]{:S(2)}, u32[]{:S(2)}) collective-permute-start(bf16[128,512]{0,1:T(8,128)(2,1)} %copy.51), channel_id=1, source_target_pairs={{0,1},{1,2},{2,3},{3,4},{4,5},{5,6},{6,7},{7,8},{8,9},{9,10},{10,1... | collective-permute-start | bytes 393224 | tf_op jit(solution)/shard_map/ppermute | solution.py:27
  219.1 2.2 copy-start.2
  219.1 2.2 copy-start.3
Sparse Core Ops, SparseCore 0:
  10.2 142.5 all-gather.1

commit v3 on v2

--- a/solution.py
+++ b/solution.py
@@ -17,7 +17,6 @@
 CAP = 8
 LANES = 128
 ROWS = 8
-GROUPS = ((0, 2), (2, 4), (4, 5))
 VMEM_BYTES = 60 * 1024 * 1024
 
 
@@ -84,75 +83,77 @@
     )(rows)
 
 
-def experts_kernel(depth, rows_ref, wide_ref, out_ref, wide, hidden, again, arrival):
+def experts_kernel(depth, rows_ref, wide_ref, out_ref, rows, wide, again, arrival):
+    slots, width = out_ref.shape
     packed = wide_ref.shape[1]
-    width = out_ref.shape[1]
     main = width // LANES * LANES
     left = width - main
+    pitch = pitch_of(depth)
     step = 2 * LANES
-    pieces = []
-    for low, high in GROUPS:
-        pieces.append((low * step, high * step))
-        pieces.append((main + low * step, main + high * step))
-    done = GROUPS[-1][1] * step
-    pieces += [(done, main), (main + done, packed)]
+    cuts = [(low, min(low + step, main)) for low in range(0, main, step)]
     copies = []
-    for place, (low, high) in enumerate(pieces):
+
+    def fetch(source, target):
+        copies.append(pltpu.make_async_copy(source, target, arrival.at[len(copies)]))
+        copies[-1].start()
+
+    def fetch_columns(low, high):
         piece = (slice(None), pl.ds(low, high - low))
-        copies.append(
-            pltpu.make_async_copy(wide_ref.at[piece], wide.at[piece], arrival.at[place])
+        fetch(wide_ref.at[piece], wide.at[piece])
+
+    fetch(rows_ref, rows)
+    for low, high in cuts:
+        fetch_columns(low, high)
+        fetch_columns(main + low, main + high)
+    fetch_columns(2 * main, packed)
+    for s in range(width // depth):
+        again[:, s * pitch + depth : (s + 1) * pitch] = jnp.zeros(
+            (slots, pitch - depth), jnp.bfloat16
         )
-        copies[-1].start()
-
-    def product(left_ref, columns):
-        return jnp.dot(left_ref[...], columns, preferred_element_type=jnp.float32)
-
-    def hidden_tiles(place, carry):
-        low = pl.multiple_of(place * step, step)
-        high = pl.multiple_of(main + place * step, LANES)
-        both = product(
-            rows_ref, jnp.concatenate([wide[:, pl.ds(low, step)], wide[:, pl.ds(high, step)]], 1)
+
+    def keep(activ, low):
+        high = low + activ.shape[1]
+        for s in range(low // depth, -(-high // depth)):
+            first, last = max(low, s * depth), min(high, (s + 1) * depth)
+            place = s * (pitch - depth)
+            again[:, first + place : last + place] = activ[:, first - low : last - low]
+
+    copies[0].wait()
+    for place, (low, high) in enumerate(cuts):
+        copies[2 * place + 1].wait()
+        copies[2 * place + 2].wait()
+        parts = [wide[:, low:high], wide[:, main + low : main + high]]
+        span = high - low
+        if high == main:
+            copies[-1].wait()
+            parts.append(wide[:, 3 * main :])
+        both = jnp.dot(
+            rows[...], jnp.concatenate(parts, 1), preferred_element_type=jnp.float32
         )
-        hidden[:, pl.ds(low, step)] = gated_hidden(both[:, :step], both[:, step:])
-        return carry
-
-    for group, (low, high) in enumerate(GROUPS):
-        copies[2 * group].wait()
-        copies[2 * group + 1].wait()
-        lax.fori_loop(low, high, hidden_tiles, 0)
-    copies[-2].wait()
-    copies[-1].wait()
-    both = product(
-        rows_ref,
-        jnp.concatenate(
-            [wide[:, done:main], wide[:, main + done : 2 * main], wide[:, 3 * main :]], 1
-        ),
-    )
-    span = main - done
-    rest = both[:, 2 * span :]
-    hidden[:, done:main] = gated_hidden(both[:, :span], both[:, span : 2 * span])
-    hidden[:, main:] = gated_hidden(rest[:, :left], rest[:, left : 2 * left])
-    spread(hidden, again, depth)
-
-    def output_tiles(place, carry):
-        low = pl.multiple_of(place * 2 * step, 2 * step)
-        source = pl.multiple_of(2 * main + place * 2 * step, LANES)
-        total = product(again, wide[:, pl.ds(source, 2 * step)])
-        out_ref[:, pl.ds(low, 2 * step)] = total.astype(jnp.bfloat16)
-        return carry
-
-    whole = main // (2 * step)
-    lax.fori_loop(0, whole, output_tiles, 0)
-    first = whole * 2 * step
-    last = product(again, wide[:, 2 * main + first :]).astype(jnp.bfloat16)
-    out_ref[:, first:main] = last[:, : main - first]
-    tail = main - first + 2 * left
-    out_ref[:, main:] = last[:, tail : tail + left]
+        keep(gated_hidden(both[:, :span], both[:, span : 2 * span]), low)
+        if high == main:
+            rest = both[:, 2 * span :]
+            keep(gated_hidden(rest[:, :left], rest[:, left : 2 * left]), main)
+
+    wider = 2 * step
+    for low in range(0, main, wider):
+        high = min(low + wider, packed - 2 * main)
+        total = jnp.dot(
+            again[...],
+            wide[:, 2 * main + low : 2 * main + high],
+            preferred_element_type=jnp.float32,
+        ).astype(jnp.bfloat16)
+        end = min(high, main)
+        out_ref[:, low:end] = total[:, : end - low]
+        if high > main:
+            tail = main - low + 2 * left
+            out_ref[:, main:] = total[:, tail : tail + left]
 
 
 def experts_call(rows, wide_all, depth, width):
     slots = rows.shape[0]
-    whole = pl.BlockSpec(memory_space=pltpu.VMEM)
+    distant = pl.BlockSpec(memory_space=pltpu.HBM)
+    tiles = -(-(width // LANES) // 2)
 
     def kernel(*refs):
         experts_kernel(depth, *refs)
@@ -160,13 +161,13 @@
     return pl.pallas_call(
         kernel,
         out_shape=jax.ShapeDtypeStruct((slots, width), jnp.bfloat16),
-        in_specs=[whole, pl.BlockSpec(memory_space=pltpu.HBM)],
-        out_specs=whole,
+        in_specs=[distant, distant],
+        out_specs=pl.BlockSpec(memory_space=pltpu.VMEM),
         scratch_shapes=[
+            pltpu.VMEM(rows.shape, jnp.bfloat16),
             pltpu.VMEM(wide_all.shape, jnp.bfloat16),
-            pltpu.VMEM((slots, width), jnp.bfloat16),
             pltpu.VMEM(rows.shape, jnp.bfloat16),
-            pltpu.SemaphoreType.DMA((2 * len(GROUPS) + 2,)),
+            pltpu.SemaphoreType.DMA((2 * tiles + 2,)),
         ],
         compiler_params=pltpu.CompilerParams(vmem_limit_bytes=VMEM_BYTES),
         cost_estimate=pl.CostEstimate(

time: 231 us -> 229 us (level)
  no operation moved by 1% of the time
where the time goes in v3:
time: 229 us; the launch traced here: 228 us
  waiting for transfers between devices  129 us (56%)
  starting transfers between devices  42.6 us (19%)
  Pallas kernels  18.2 us (8%)
  between operations  14.4 us (6%)
  local copies, waits for them, and re-layouts  13.5 us (6%)
  other arithmetic  5.53 us (2%)
  matrix products  5.15 us (2%)
    all_to_all x4, waiting for transfers between devices, exchange(): lax.all_to_all(parts, 'exp', split_axis=0, concat_axis=0, tiled=True)  49.9 us
    all_gather x1, waiting for transfers between devices, per_device(): wide_all = lax.all_gather(wide, 'ctx', axis=0, tiled=True)  49.8 us
    all_to_all x4, starting transfers between devices, exchange(): lax.all_to_all(parts, 'exp', split_axis=0, concat_axis=0, tiled=True)  40.3 us
    ppermute x1, waiting for transfers between devices, shifted(): return lax.ppermute(block, axis, route)  29.2 us
    pallas_call x1, Pallas kernels, experts_call(): pl.pallas_call(kernel, out_shape=jax.ShapeDtypeStruct((slots, width), jnp...  12.1 us
  transfers between devices with their start and end apart: 6, of which 4 were waited for; matrix products, arithmetic and copies ran while one was open for 10% of the time, Pallas kernels for 7%

profile of v3, /device:TPU:6, one launch (start us, length us, event | category | flops | bytes accessed | tf_op | source)
XLA Modules:
  0.0 228.2 jit_solution(2589855715629119633)
XLA Ops:
  7.2 2.8 %shard_map.132 = bf16[184,4352]{1,0:T(8,128)(2,1)} custom-call(bf16[180,1440]{1,0:T(8,128)(2,1)} %bitcast.55, bf16[180,1440]{1,0:T(8,128)(2,1)} %bitcast.56, bf16[180,1440]{1,0:T(8,128)(2,1)} %bitcast.57), custom_call_target="tpu_custom_call" | custom-call | bytes 3110400 | tf_op jit(solution)/shard_map/pallas_call | solution.py:53
  10.5 0.9 reshape.87
  11.4 14.0 %all-to-all-start = ((bf16[64,2,1440]{2,1,0:T(2,128)(2,1)}), bf16[64,2,1440]{2,1,0:T(2,128)(2,1)S(1)}, u32[]{:S(2)}, u32[]{:S(2)}) async-start(bf16[64,2,1440]{2,1,0:T(2,128)(2,1)} %reshape.87), calls=%async_computation | async-start | bytes 786432 | tf_op jit(solution)/shard_map/all_to_all | solution.py:183
  26.2 13.4 %all-to-all-done = bf16[64,2,1440]{2,1,0:T(2,128)(2,1)S(1)} async-done(((bf16[64,2,1440]{2,1,0:T(2,128)(2,1)}), bf16[64,2,1440]{2,1,0:T(2,128)(2,1)S(1)}, u32[]{:S(2)}, u32[]{:S(2)}) %all-to-all-start) | async-done | bytes 368672 | tf_op jit(solution)/shard_map/all_to_all | solution.py:183
  39.6 0.5 multiply_reduce_fusion
  40.5 0.7 convolution_convert_fusion.1
  41.2 1.6 copy.42
  42.8 6.8 %all-to-all-start.1 = ((bf16[64,8,1440]{2,1,0:T(8,128)(2,1)}), bf16[64,8,1440]{2,1,0:T(8,128)(2,1)S(1)}, u32[]{:S(2)}, u32[]{:S(2)}) async-start(bf16[64,8,1440]{2,1,0:T(8,128)(2,1)} %bitcast.52), calls=%async_computation.1 | async-start | bytes 3145728 | tf_op jit(solution)/shard_map/all_to_all | solution.py:183
  49.6 1.1 pad_maximum_fusion
  50.7 36.5 %all-to-all-done.1 = bf16[64,8,1440]{2,1,0:T(8,128)(2,1)S(1)} async-done(((bf16[64,8,1440]{2,1,0:T(8,128)(2,1)}), bf16[64,8,1440]{2,1,0:T(8,128)(2,1)S(1)}, u32[]{:S(2)}, u32[]{:S(2)}) %all-to-all-start.1) | async-done | bytes 1474592 | tf_op jit(solution)/shard_map/all_to_all | solution.py:183
  87.2 1.3 convolution_convert_fusion
  88.5 2.6 %reshape.90 = bf16[64,2,2560]{2,1,0:T(2,128)(2,1)} reshape(bf16[128,2560]{1,0:T(8,128)(2,1)} %convolution_convert_fusion) | data formatting | bytes 1310720 | tf_op jit(solution)/shard_map/reshape | solution.py:182
  91.2 8.4 %all-to-all-start.2 = ((bf16[64,2,2560]{2,1,0:T(2,128)(2,1)}), bf16[64,2,2560]{2,1,0:T(2,128)(2,1)S(1)}, u32[]{:S(2)}, u32[]{:S(2)}) async-start(bf16[64,2,2560]{2,1,0:T(2,128)(2,1)} %reshape.90), calls=%async_computation.2 | async-start | bytes 1310720 | tf_op jit(solution)/shard_map/all_to_all | solution.py:183
  99.7 3.3 %shard_map.131.refs_0_ = bf16[512,1472]{1,0:T(8,128)(2,1)} custom-call(bf16[512,1440]{1,0:T(8,128)(2,1)} %bitcast.51), custom_call_target="tpu_custom_call" | custom-call | bytes 2949120 | tf_op jit(solution)/shard_map/pallas_call | solution.py:77
  103.0 49.8 %all-gather.2.cloned.1.call-done.refs_1_ = bf16[1472,4352]{1,0:T(8,128)(2,1)} async-done(((bf16[184,4352]{1,0:T(8,128)(2,1)}), bf16[1472,4352]{1,0:T(8,128)(2,1)}) %all-gather.2.cloned.1.call-update) | async-done | bytes 12812304 | tf_op jit(solution)/shard_map/all_gather | solution.py:238
  152.7 12.1 %shard_map.133 = bf16[512,1440]{1,0:T(8,128)(2,1)} custom-call(bf16[512,1472]{1,0:T(8,128)(2,1)} %shard_map.131.refs_0_, bf16[1472,4352]{1,0:T(8,128)(2,1)} %all-gather.2.cloned.1.call-done.refs_1_), custom_call_target="tpu_custom_call" | custom-call | flops 6370099200 | bytes 15390720 | tf_op jit(solution)/shard_map/pallas_call | solution.py:161
  164.9 11.1 %all-to-all-start.3 = ((bf16[64,8,1440]{2,1,0:T(8,128)(2,1)}), bf16[64,8,1440]{2,1,0:T(8,128)(2,1)S(1)}, u32[]{:S(2)}, u32[]{:S(2)}) async-start(bf16[64,8,1440]{2,1,0:T(8,128)(2,1)} %bitcast.54), calls=%async_computation.3 | async-start | bytes 3145728 | tf_op jit(solution)/shard_map/all_to_all | solution.py:183
  176.0 0.9 add_convert_fusion.1
  176.9 1.1 reshape.91
  178.0 0.9 slice.52
  178.9 0.8 copy.51
  179.7 2.3 collective-permute-start
  182.3 1.9 slice.55
  184.2 1.3 copy.52
  185.6 29.2 %collective-permute-done = bf16[128,512]{0,1:T(8,128)(2,1)} collective-permute-done((bf16[128,512]{0,1:T(8,128)(2,1)}, bf16[128,512]{0,1:T(8,128)(2,1)}, u32[]{:S(2)}, u32[]{:S(2)}) %collective-permute-start) | collective-permute-done | bytes 131104 | tf_op jit(solution)/shard_map/ppermute | solution.py:26
  214.7 1.0 pad_maximum_fusion.1
  215.7 0.8 fusion.1
  216.5 0.9 fusion
  217.5 1.2 fusion.5
  218.7 1.0 copy.47
  219.8 0.8 fusion.3
  220.5 0.9 fusion.8
  (50 shorter events, 2.3 us)
Async XLA Ops:
  7.2 2.9 %copy-start = (bf16[128,1440]{0,1:T(8,128)(2,1)S(1)}, bf16[128,1440]{0,1:T(8,128)(2,1)}, u32[]{:S(2)}) copy-start(bf16[128,1440]{0,1:T(8,128)(2,1)} %param.12) | copy-start | bytes 1105924
  7.2 2.9 %copy-start.10 = (s32[128]{0:T(128)S(1)}, s32[128]{0:T(128)}, u32[]{:S(2)}) copy-start(s32[128]{0:T(128)} %param.18) | copy-start | bytes 1540
  7.2 18.3 %copy-start.7 = (s32[128,2]{0,1:T(2,128)S(1)}, s32[128,2]{0,1:T(2,128)}, u32[]{:S(2)}) copy-start(s32[128,2]{0,1:T(2,128)} %param.19) | copy-start | bytes 3076
  7.2 145.5 %all-gather.2.cloned.1.call-start = ((), (), s32[]{:S(2)}) async-start(), calls=%async_computation.4 | async-start | bytes 14413824 | tf_op jit(solution)/shard_map/all_gather | solution.py:238
  10.0 30.5 %copy-start.6 = (f32[1440]{0:T(1024)S(1)}, f32[1440]{0:T(1024)}, u32[]{:S(2)}) copy-start(f32[1440]{0:T(1024)} %param.17) | copy-start | bytes 17284
  11.4 28.2 %all-to-all-start = ((bf16[64,2,1440]{2,1,0:T(2,128)(2,1)}), bf16[64,2,1440]{2,1,0:T(2,128)(2,1)S(1)}, u32[]{:S(2)}, u32[]{:S(2)}) async-start(bf16[64,2,1440]{2,1,0:T(2,128)(2,1)} %reshape.87), calls=%async_computation | async-start | bytes 786432 | tf_op jit(solution)/shard_map/all_to_all | solution.py:183
  40.5 9.1 %copy-start.4 = (bf16[128,256]{1,0:T(8,128)(2,1)S(1)}, bf16[128,256]{1,0:T(8,128)(2,1)}, u32[]{:S(2)}) copy-start(bf16[128,256]{1,0:T(8,128)(2,1)} %param.15) | copy-start | bytes 196612
  40.5 9.1 %copy-start.5 = (bf16[128,256]{1,0:T(8,128)(2,1)S(1)}, bf16[128,256]{1,0:T(8,128)(2,1)}, u32[]{:S(2)}) copy-start(bf16[128,256]{1,0:T(8,128)(2,1)} %param.14) | copy-start | bytes 196612
  42.8 56.8 %copy-start.9 = (f32[32]{0:T(128)S(1)}, f32[32]{0:T(128)}, u32[]{:S(2)}) copy-start(f32[32]{0:T(128)} %param.16) | copy-start | bytes 388
  42.8 44.4 %all-to-all-start.1 = ((bf16[64,8,1440]{2,1,0:T(8,128)(2,1)}), bf16[64,8,1440]{2,1,0:T(8,128)(2,1)S(1)}, u32[]{:S(2)}, u32[]{:S(2)}) async-start(bf16[64,8,1440]{2,1,0:T(8,128)(2,1)} %bitcast.52), calls=%async_computation.1 | async-start | bytes 3145728 | tf_op jit(solution)/shard_map/all_to_all | solution.py:183
  87.2 12.5 %copy-start.1 = (bf16[64,8,1440]{2,1,0:T(8,128)(2,1)}, bf16[64,8,1440]{2,1,0:T(8,128)(2,1)S(1)}, u32[]{:S(2)}) copy-start(bf16[64,8,1440]{2,1,0:T(8,128)(2,1)S(1)} %all-to-all-done.1) | copy-start | bytes 4423684
  91.2 73.7 %all-to-all-start.2 = ((bf16[64,2,2560]{2,1,0:T(2,128)(2,1)}), bf16[64,2,2560]{2,1,0:T(2,128)(2,1)S(1)}, u32[]{:S(2)}, u32[]{:S(2)}) async-start(bf16[64,2,2560]{2,1,0:T(2,128)(2,1)} %reshape.90), calls=%async_computation.2 | async-start | bytes 1310720 | tf_op jit(solution)/shard_map/all_to_all | solution.py:183
  103.0 73.1 %copy-start.8 = (f32[128,2]{0,1:T(2,128)S(1)}, f32[128,2]{0,1:T(2,128)}, u32[]{:S(2)}) copy-start(f32[128,2]{0,1:T(2,128)} %param.20) | copy-start | bytes 3076
  164.9 54.9 %all-to-all-start.3 = ((bf16[64,8,1440]{2,1,0:T(8,128)(2,1)}), bf16[64,8,1440]{2,1,0:T(8,128)(2,1)S(1)}, u32[]{:S(2)}, u32[]{:S(2)}) async-start(bf16[64,8,1440]{2,1,0:T(8,128)(2,1)} %bitcast.54), calls=%async_computation.3 | async-start | bytes 3145728 | tf_op jit(solution)/shard_map/all_to_all | solution.py:183
  179.7 35.1 %collective-permute-start = (bf16[128,512]{0,1:T(8,128)(2,1)}, bf16[128,512]{0,1:T(8,128)(2,1)}, u32[]{:S(2)}, u32[]{:S(2)}) collective-permute-start(bf16[128,512]{0,1:T(8,128)(2,1)} %copy.51), channel_id=1, source_target_pairs={{0,1},{1,2},{2,3},{3,4},{4,5},{5,6},{6,7},{7,8},{8,9},{9,10},{10,1... | collective-permute-start | bytes 393224 | tf_op jit(solution)/shard_map/ppermute | solution.py:26
  217.5 2.2 copy-start.2
  217.5 2.2 copy-start.3
Sparse Core Ops, SparseCore 0:
  10.2 142.5 all-gather.1

commit v4 on v3

--- a/solution.py
+++ b/solution.py
@@ -90,7 +90,8 @@
     left = width - main
     pitch = pitch_of(depth)
     step = 2 * LANES
-    cuts = [(low, min(low + step, main)) for low in range(0, main, step)]
+    lead = main % step
+    cuts = [(max(low, 0), low + step) for low in range(lead - step, main, step)]
     copies = []
 
     def fetch(source, target):
@@ -153,7 +154,7 @@
 def experts_call(rows, wide_all, depth, width):
     slots = rows.shape[0]
     distant = pl.BlockSpec(memory_space=pltpu.HBM)
-    tiles = -(-(width // LANES) // 2)
+    tiles = width // LANES // 2 + 1
 
     def kernel(*refs):
         experts_kernel(depth, *refs)
@@ -184,7 +185,7 @@
 
 
 def gated_hidden(gate, upward):
-    return (gate * jax.nn.sigmoid(1.702 * gate) * (upward + 1.0)).astype(jnp.bfloat16)
+    return (gate * (0.5 + 0.5 * jnp.tanh(0.851 * gate)) * (upward + 1.0)).astype(jnp.bfloat16)
 
 
 def attend(query_rows, key_value_rows, sinks):

time: 229 us -> 230 us (level)
  no operation moved by 1% of the time
where the time goes in v4:
time: 230 us; the launch traced here: 229 us
  waiting for transfers between devices  129 us (56%)
  starting transfers between devices  42.6 us (19%)
  Pallas kernels  18.8 us (8%)
  between operations  14.4 us (6%)
  local copies, waits for them, and re-layouts  13.5 us (6%)
  other arithmetic  5.53 us (2%)
  matrix products  5.15 us (2%)
    all_to_all x4, waiting for transfers between devices, exchange(): lax.all_to_all(parts, 'exp', split_axis=0, concat_axis=0, tiled=True)  49.9 us
    all_gather x1, waiting for transfers between devices, per_device(): wide_all = lax.all_gather(wide, 'ctx', axis=0, tiled=True)  49.8 us
    all_to_all x4, starting transfers between devices, exchange(): lax.all_to_all(parts, 'exp', split_axis=0, concat_axis=0, tiled=True)  40.3 us
    ppermute x1, waiting for transfers between devices, shifted(): return lax.ppermute(block, axis, route)  29.2 us
    pallas_call x1, Pallas kernels, experts_call(): pl.pallas_call(kernel, out_shape=jax.ShapeDtypeStruct((slots, width), jnp...  12.7 us
  transfers between devices with their start and end apart: 6, of which 4 were waited for; matrix products, arithmetic and copies ran while one was open for 10% of the time, Pallas kernels for 7%

profile of v4, /device:TPU:6, one launch (start us, length us, event | category | flops | bytes accessed | tf_op | source)
XLA Modules:
  0.0 228.8 jit_solution(15084004929591945971)
XLA Ops:
  7.2 2.8 %shard_map.132 = bf16[184,4352]{1,0:T(8,128)(2,1)} custom-call(bf16[180,1440]{1,0:T(8,128)(2,1)} %bitcast.55, bf16[180,1440]{1,0:T(8,128)(2,1)} %bitcast.56, bf16[180,1440]{1,0:T(8,128)(2,1)} %bitcast.57), custom_call_target="tpu_custom_call" | custom-call | bytes 3110400 | tf_op jit(solution)/shard_map/pallas_call | solution.py:53
  10.5 0.9 reshape.87
  11.4 14.0 %all-to-all-start = ((bf16[64,2,1440]{2,1,0:T(2,128)(2,1)}), bf16[64,2,1440]{2,1,0:T(2,128)(2,1)S(1)}, u32[]{:S(2)}, u32[]{:S(2)}) async-start(bf16[64,2,1440]{2,1,0:T(2,128)(2,1)} %reshape.87), calls=%async_computation | async-start | bytes 786432 | tf_op jit(solution)/shard_map/all_to_all | solution.py:184
  26.2 13.4 %all-to-all-done = bf16[64,2,1440]{2,1,0:T(2,128)(2,1)S(1)} async-done(((bf16[64,2,1440]{2,1,0:T(2,128)(2,1)}), bf16[64,2,1440]{2,1,0:T(2,128)(2,1)S(1)}, u32[]{:S(2)}, u32[]{:S(2)}) %all-to-all-start) | async-done | bytes 368672 | tf_op jit(solution)/shard_map/all_to_all | solution.py:184
  39.6 0.5 multiply_reduce_fusion
  40.5 0.7 convolution_convert_fusion.1
  41.2 1.6 copy.42
  42.8 6.8 %all-to-all-start.1 = ((bf16[64,8,1440]{2,1,0:T(8,128)(2,1)}), bf16[64,8,1440]{2,1,0:T(8,128)(2,1)S(1)}, u32[]{:S(2)}, u32[]{:S(2)}) async-start(bf16[64,8,1440]{2,1,0:T(8,128)(2,1)} %bitcast.52), calls=%async_computation.1 | async-start | bytes 3145728 | tf_op jit(solution)/shard_map/all_to_all | solution.py:184
  49.6 1.1 pad_maximum_fusion
  50.7 36.5 %all-to-all-done.1 = bf16[64,8,1440]{2,1,0:T(8,128)(2,1)S(1)} async-done(((bf16[64,8,1440]{2,1,0:T(8,128)(2,1)}), bf16[64,8,1440]{2,1,0:T(8,128)(2,1)S(1)}, u32[]{:S(2)}, u32[]{:S(2)}) %all-to-all-start.1) | async-done | bytes 1474592 | tf_op jit(solution)/shard_map/all_to_all | solution.py:184
  87.2 1.3 convolution_convert_fusion
  88.5 2.6 %reshape.90 = bf16[64,2,2560]{2,1,0:T(2,128)(2,1)} reshape(bf16[128,2560]{1,0:T(8,128)(2,1)} %convolution_convert_fusion) | data formatting | bytes 1310720 | tf_op jit(solution)/shard_map/reshape | solution.py:183
  91.2 8.4 %all-to-all-start.2 = ((bf16[64,2,2560]{2,1,0:T(2,128)(2,1)}), bf16[64,2,2560]{2,1,0:T(2,128)(2,1)S(1)}, u32[]{:S(2)}, u32[]{:S(2)}) async-start(bf16[64,2,2560]{2,1,0:T(2,128)(2,1)} %reshape.90), calls=%async_computation.2 | async-start | bytes 1310720 | tf_op jit(solution)/shard_map/all_to_all | solution.py:184
  99.7 3.3 %shard_map.131.refs_0_ = bf16[512,1472]{1,0:T(8,128)(2,1)} custom-call(bf16[512,1440]{1,0:T(8,128)(2,1)} %bitcast.51), custom_call_target="tpu_custom_call" | custom-call | bytes 2949120 | tf_op jit(solution)/shard_map/pallas_call | solution.py:77
  103.0 49.8 %all-gather.2.cloned.1.call-done.refs_1_ = bf16[1472,4352]{1,0:T(8,128)(2,1)} async-done(((bf16[184,4352]{1,0:T(8,128)(2,1)}), bf16[1472,4352]{1,0:T(8,128)(2,1)}) %all-gather.2.cloned.1.call-update) | async-done | bytes 12812304 | tf_op jit(solution)/shard_map/all_gather | solution.py:239
  152.7 12.7 %shard_map.133 = bf16[512,1440]{1,0:T(8,128)(2,1)} custom-call(bf16[512,1472]{1,0:T(8,128)(2,1)} %shard_map.131.refs_0_, bf16[1472,4352]{1,0:T(8,128)(2,1)} %all-gather.2.cloned.1.call-done.refs_1_), custom_call_target="tpu_custom_call" | custom-call | flops 6370099200 | bytes 15390720 | tf_op jit(solution)/shard_map/pallas_call | solution.py:162
  165.4 11.1 %all-to-all-start.3 = ((bf16[64,8,1440]{2,1,0:T(8,128)(2,1)}), bf16[64,8,1440]{2,1,0:T(8,128)(2,1)S(1)}, u32[]{:S(2)}, u32[]{:S(2)}) async-start(bf16[64,8,1440]{2,1,0:T(8,128)(2,1)} %bitcast.54), calls=%async_computation.3 | async-start | bytes 3145728 | tf_op jit(solution)/shard_map/all_to_all | solution.py:184
  176.6 0.9 add_convert_fusion.1
  177.5 1.1 reshape.91
  178.5 0.9 slice.52
  179.5 0.8 copy.51
  180.2 2.3 collective-permute-start
  182.9 1.9 slice.55
  184.8 1.3 copy.52
  186.1 29.2 %collective-permute-done = bf16[128,512]{0,1:T(8,128)(2,1)} collective-permute-done((bf16[128,512]{0,1:T(8,128)(2,1)}, bf16[128,512]{0,1:T(8,128)(2,1)}, u32[]{:S(2)}, u32[]{:S(2)}) %collective-permute-start) | collective-permute-done | bytes 131104 | tf_op jit(solution)/shard_map/ppermute | solution.py:26
  215.3 1.0 pad_maximum_fusion.1
  216.3 0.8 fusion.1
  217.1 0.9 fusion
  218.1 1.2 fusion.5
  219.3 1.0 copy.47
  220.3 0.8 fusion.3
  221.1 0.9 fusion.8
  (50 shorter events, 2.3 us)
Async XLA Ops:
  7.2 2.9 %copy-start = (bf16[128,1440]{0,1:T(8,128)(2,1)S(1)}, bf16[128,1440]{0,1:T(8,128)(2,1)}, u32[]{:S(2)}) copy-start(bf16[128,1440]{0,1:T(8,128)(2,1)} %param.12) | copy-start | bytes 1105924
  7.2 2.9 %copy-start.10 = (s32[128]{0:T(128)S(1)}, s32[128]{0:T(128)}, u32[]{:S(2)}) copy-start(s32[128]{0:T(128)} %param.18) | copy-start | bytes 1540
  7.2 18.3 %copy-start.7 = (s32[128,2]{0,1:T(2,128)S(1)}, s32[128,2]{0,1:T(2,128)}, u32[]{:S(2)}) copy-start(s32[128,2]{0,1:T(2,128)} %param.19) | copy-start | bytes 3076
  7.2 145.5 %all-gather.2.cloned.1.call-start = ((), (), s32[]{:S(2)}) async-start(), calls=%async_computation.4 | async-start | bytes 14413824 | tf_op jit(solution)/shard_map/all_gather | solution.py:239
  10.0 30.5 %copy-start.6 = (f32[1440]{0:T(1024)S(1)}, f32[1440]{0:T(1024)}, u32[]{:S(2)}) copy-start(f32[1440]{0:T(1024)} %param.17) | copy-start | bytes 17284
  11.4 28.2 %all-to-all-start = ((bf16[64,2,1440]{2,1,0:T(2,128)(2,1)}), bf16[64,2,1440]{2,1,0:T(2,128)(2,1)S(1)}, u32[]{:S(2)}, u32[]{:S(2)}) async-start(bf16[64,2,1440]{2,1,0:T(2,128)(2,1)} %reshape.87), calls=%async_computation | async-start | bytes 786432 | tf_op jit(solution)/shard_map/all_to_all | solution.py:184
  40.5 9.1 %copy-start.4 = (bf16[128,256]{1,0:T(8,128)(2,1)S(1)}, bf16[128,256]{1,0:T(8,128)(2,1)}, u32[]{:S(2)}) copy-start(bf16[128,256]{1,0:T(8,128)(2,1)} %param.15) | copy-start | bytes 196612
  40.5 9.1 %copy-start.5 = (bf16[128,256]{1,0:T(8,128)(2,1)S(1)}, bf16[128,256]{1,0:T(8,128)(2,1)}, u32[]{:S(2)}) copy-start(bf16[128,256]{1,0:T(8,128)(2,1)} %param.14) | copy-start | bytes 196612
  42.8 56.8 %copy-start.9 = (f32[32]{0:T(128)S(1)}, f32[32]{0:T(128)}, u32[]{:S(2)}) copy-start(f32[32]{0:T(128)} %param.16) | copy-start | bytes 388
  42.8 44.4 %all-to-all-start.1 = ((bf16[64,8,1440]{2,1,0:T(8,128)(2,1)}), bf16[64,8,1440]{2,1,0:T(8,128)(2,1)S(1)}, u32[]{:S(2)}, u32[]{:S(2)}) async-start(bf16[64,8,1440]{2,1,0:T(8,128)(2,1)} %bitcast.52), calls=%async_computation.1 | async-start | bytes 3145728 | tf_op jit(solution)/shard_map/all_to_all | solution.py:184
  87.2 12.5 %copy-start.1 = (bf16[64,8,1440]{2,1,0:T(8,128)(2,1)}, bf16[64,8,1440]{2,1,0:T(8,128)(2,1)S(1)}, u32[]{:S(2)}) copy-start(bf16[64,8,1440]{2,1,0:T(8,128)(2,1)S(1)} %all-to-all-done.1) | copy-start | bytes 4423684
  91.2 74.3 %all-to-all-start.2 = ((bf16[64,2,2560]{2,1,0:T(2,128)(2,1)}), bf16[64,2,2560]{2,1,0:T(2,128)(2,1)S(1)}, u32[]{:S(2)}, u32[]{:S(2)}) async-start(bf16[64,2,2560]{2,1,0:T(2,128)(2,1)} %reshape.90), calls=%async_computation.2 | async-start | bytes 1310720 | tf_op jit(solution)/shard_map/all_to_all | solution.py:184
  103.0 73.6 %copy-start.8 = (f32[128,2]{0,1:T(2,128)S(1)}, f32[128,2]{0,1:T(2,128)}, u32[]{:S(2)}) copy-start(f32[128,2]{0,1:T(2,128)} %param.20) | copy-start | bytes 3076
  165.4 54.9 %all-to-all-start.3 = ((bf16[64,8,1440]{2,1,0:T(8,128)(2,1)}), bf16[64,8,1440]{2,1,0:T(8,128)(2,1)S(1)}, u32[]{:S(2)}, u32[]{:S(2)}) async-start(bf16[64,8,1440]{2,1,0:T(8,128)(2,1)} %bitcast.54), calls=%async_computation.3 | async-start | bytes 3145728 | tf_op jit(solution)/shard_map/all_to_all | solution.py:184
  180.2 35.1 %collective-permute-start = (bf16[128,512]{0,1:T(8,128)(2,1)}, bf16[128,512]{0,1:T(8,128)(2,1)}, u32[]{:S(2)}, u32[]{:S(2)}) collective-permute-start(bf16[128,512]{0,1:T(8,128)(2,1)} %copy.51), channel_id=1, source_target_pairs={{0,1},{1,2},{2,3},{3,4},{4,5},{5,6},{6,7},{7,8},{8,9},{9,10},{10,1... | collective-permute-start | bytes 393224 | tf_op jit(solution)/shard_map/ppermute | solution.py:26
  218.1 2.2 copy-start.2
  218.1 2.2 copy-start.3
Sparse Core Ops, SparseCore 0:
  10.2 142.5 all-gather.1
